TPU v7x, 512 devices: a whole 4x4x16 slice. The times are simulated.
512 devices in a mesh: pipe: 32 (over x_lo, z), tensor: 4 (over y), dp: 4 (over x_hi, core).
Axes of the slice: x: 4 (x_hi: 2, x_lo: 2; x = x_hi * 2 + x_lo), y: 4, z: 16, core: 2. Of those that a mesh axis runs over, the one named last changes fastest.
Arguments:
- grad_in: bfloat16 [32, 4, 128, 8192], P('pipe', 'dp', 'tensor'), may hold values from -6 to 6
- saved_x: bfloat16 [32, 4, 3, 128, 8192], P('pipe', 'dp', None, None, 'tensor'), may hold values from -6 to 6
- saved_z: bfloat16 [32, 4, 3, 128, 8192], P('pipe', 'dp', None, None, 'tensor'), may hold values from -6 to 6
- saved_dt: float32 [32, 4, 3, 128, 128], P('pipe', 'dp', None, None, 'tensor'), may hold values from 0.5 to 1.5
- saved_b: bfloat16 [32, 4, 3, 128, 8, 128], P('pipe', 'dp', None, None, 'tensor'), may hold values from -0.5 to 0.5
- saved_c: bfloat16 [32, 4, 3, 128, 8, 128], P('pipe', 'dp', None, None, 'tensor'), may hold values from -6 to 6
- a_log: float32 [32, 2, 128], P('pipe', None, 'tensor'), may hold values from -6.2 to -3
- dskip: float32 [32, 2, 128], P('pipe', None, 'tensor'), may hold values from 0.5 to 1.5
- gain: float32 [32, 2, 8192], P('pipe', None, 'tensor'), may hold values from 0.5 to 1.5
- block_table: int32 [2, 32, 4], P(None, 'pipe', 'dp'), may hold values from 0 to 1
- entry_table: int32 [2, 32, 4], P(None, 'pipe', 'dp'), may hold values from 0 to 2
Outputs:
- grad_out: bfloat16 [32, 4, 128, 8192], P('pipe', 'dp', 'tensor')
- grad_alog: float32 [32, 2, 128], P('pipe', None, ('tensor', 'dp'))
- grad_dskip: float32 [32, 2, 128], P('pipe', None, ('tensor', 'dp'))
- grad_gain: float32 [32, 2, 8192], P('pipe', None, ('tensor', 'dp'))
All inputs are finite; a program needn't handle non-finite values.
Results may differ from a plain program's by a relative error of at most 0.023.
Values may be sent and summed in bfloat16 or wider, within the bound.
No kernel may reach another device: no remote copies, remote signals or barrier semaphores. Data moves between devices by JAX's collectives and lax.ppermute only.
A program may use at most 64 MiB of HBM per device.

v0:
```python
from functools import partial

import jax
import jax.numpy as jnp
from jax import lax
from jax.experimental import pallas as pl
from jax.experimental.pallas import tpu as pltpu
from jax.sharding import PartitionSpec as P

eps = 1e-05
f32 = jnp.float32
bf16 = jnp.bfloat16
LANES = 128


def passed_along(block, axis, distance):
    devices = range(lax.axis_size(axis))
    route = [((i - distance) % len(devices), i) for i in devices]
    return lax.ppermute(block, axis, route)


def thirds(value):
    high = value.astype(bf16)
    rest = value - high.astype(f32)
    middle = rest.astype(bf16)
    return high, middle, (rest - middle.astype(f32)).astype(bf16)


def of_block(ref, block, here=slice(None)):
    rows = ref[0, :, here]
    row = rows[0:1]
    for other in range(1, rows.shape[0]):
        row = jnp.where(block == other, rows[other : other + 1], row)
    return row


def spread_map(heads, width):
    head = lax.broadcasted_iota(jnp.int32, (3 * heads, heads * width), 0) % heads
    lane = lax.broadcasted_iota(jnp.int32, (3 * heads, heads * width), 1)
    return (lane // width == head).astype(bf16)


def spread(values, one_hot):
    return jnp.dot(jnp.concatenate(thirds(values), axis=1), one_hot, preferred_element_type=f32)


def halves(value):
    high = value.astype(bf16)
    return high, (value - high.astype(f32)).astype(bf16)


def forward(
    tick,
    block_ref,
    entry_ref,
    x_hbm,
    z_hbm,
    dt_hbm,
    b_hbm,
    c_hbm,
    alog_ref,
    dskip_ref,
    gain_ref,
    x_ref,
    slope_ref,
    normed_ref,
    scores_ref,
    heads_ref,
    rows_ref,
    z_ref,
    dt_ref,
    b_ref,
    c_ref,
    drive_ref,
    wx_ref,
    ec_ref,
    y_ref,
    gated_ref,
    gate_ref,
    sem,
):
    block = block_ref[tick]
    entry = entry_ref[tick]
    moves = [
        pltpu.make_async_copy(src.at[0, 0, entry], dst, sem.at[i])
        for i, (src, dst) in enumerate(
            ((dt_hbm, dt_ref), (b_hbm, b_ref), (c_hbm, c_ref), (x_hbm, x_ref), (z_hbm, z_ref))
        )
    ]
    for move in moves:
        move.start()
    seq, chan = normed_ref.shape
    groups = scores_ref.shape[0]
    heads = dt_ref.shape[0]
    width = chan // heads
    per_group = chan // groups
    held = heads // groups
    tiles = per_group // LANES
    row = lax.broadcasted_iota(jnp.int32, (seq, seq), 0)
    col = lax.broadcasted_iota(jnp.int32, (seq, seq), 1)
    rate = jnp.exp(of_block(alog_ref, block))
    one_hot = spread_map(held, width)
    rows_ref[0:1] = of_block(gain_ref, block)
    skips = jnp.broadcast_to(of_block(dskip_ref, block), (8, heads))
    for group in range(groups):
        mine = slice(group * held, (group + 1) * held)
        rows_ref[1:2, pl.ds(group * per_group, per_group)] = spread(skips[:, mine], one_hot)[0:1]
    moves[0].wait()
    lower = (row >= col).astype(bf16)
    same = (row == col).astype(bf16)
    taken = jnp.concatenate([jnp.concatenate([lower] * 3, axis=1), jnp.concatenate([same] * 3, axis=1)], axis=0)
    steps = jnp.concatenate(thirds(dt_ref[...]), axis=1)
    steps = lax.dot_general(taken, steps, (((1,), (1,)), ((), ())), preferred_element_type=f32)
    cum = -steps[0:seq] * rate
    grow = jnp.exp(-cum)
    fall = jnp.exp(cum)
    weight = grow * steps[seq:]
    heads_ref[:, 0:heads] = cum
    heads_ref[:, heads : 2 * heads] = grow
    heads_ref[:, 2 * heads : 3 * heads] = weight
    for group in range(groups):
        mine = slice(group * held, (group + 1) * held)
        both = spread(jnp.concatenate([weight[:, mine], fall[:, mine]], axis=0), one_hot)
        wx_ref[group] = both[0:seq]
        ec_ref[group] = both[seq:]
    moves[1].wait()
    moves[2].wait()
    mixers = []
    for group in range(groups):
        bmat = b_ref[:, group, :]
        cmat = c_ref[:, group, :]
        st = lax.dot_general(bmat, cmat, (((1,), (1,)), ((), ())), preferred_element_type=f32)
        scores_ref[group, 1], scores_ref[group, 2] = halves(jnp.where(row <= col, st, 0.0))
        scores = lax.dot_general(cmat, bmat, (((1,), (1,)), ((), ())), preferred_element_type=f32)
        high, low = halves(jnp.where(row >= col, scores, 0.0))
        scores_ref[group, 0] = high
        mixers.append(jnp.concatenate([high, high, low], axis=1))
    moves[3].wait()
    for group in range(groups):
        for tile in range(tiles):
            here = pl.ds(group * per_group + tile * LANES, LANES)
            there = pl.ds(tile * LANES, LANES)
            high, low = halves(wx_ref[group, :, there] * x_ref[:, here].astype(f32))
            drive_ref[group, 0:seq, there] = high
            drive_ref[group, seq : 2 * seq, there] = low
            drive_ref[group, 2 * seq :, there] = high
        y_ref[group] = jnp.dot(mixers[group], drive_ref[group], preferred_element_type=f32)
    moves[4].wait()
    for group in range(groups):
        total = jnp.zeros((seq, LANES), f32)
        for tile in range(tiles):
            here = pl.ds(group * per_group + tile * LANES, LANES)
            there = pl.ds(tile * LANES, LANES)
            ec = ec_ref[group, :, there]
            z = z_ref[:, here].astype(f32)
            gate = z * jax.nn.sigmoid(z)
            gated = (ec * y_ref[group, :, there] + rows_ref[1:2, here] * x_ref[:, here].astype(f32)) * gate
            total = total + gated * gated
            gated_ref[group, :, there] = gated
            gate_ref[group, :, there] = ec * gate
        scale = lax.rsqrt(jnp.sum(total, axis=1, keepdims=True) * (1.0 / per_group) + eps)
        for tile in range(tiles):
            here = pl.ds(group * per_group + tile * LANES, LANES)
            there = pl.ds(tile * LANES, LANES)
            normed_ref[:, here] = (gated_ref[group, :, there] * scale).astype(bf16)
            slope_ref[:, here] = gate_ref[group, :, there] * scale


def backward(g_ref, x_ref, slope_ref, normed_ref, scores_ref, heads_ref, rows_ref, scratch, dx_ref, want_rows):
    drive_ref, v_ref, q_ref, y_ref, part_ref, wide_ref = scratch
    seq, chan = normed_ref.shape
    groups = scores_ref.shape[0]
    heads = heads_ref.shape[1] // 3
    per_group = chan // groups
    held = heads // groups
    width = per_group // held
    tiles = per_group // LANES
    one_hot = spread_map(held, width)
    found = [[], [], []]
    means = []
    for group in range(groups):
        total = jnp.zeros((seq, LANES), f32)
        for tile in range(tiles):
            here = pl.ds(group * per_group + tile * LANES, LANES)
            gn = g_ref[:, here].astype(f32) * normed_ref[:, here].astype(f32)
            total = total + gn * rows_ref[0:1, here]
            if want_rows:
                found[0].append(jnp.sum(gn, axis=0, keepdims=True))
        means.append(jnp.sum(total, axis=1, keepdims=True) * (1.0 / per_group))
        kinds = range(3) if want_rows else range(1, 3)
        factors = [heads_ref[:, kind * heads + group * held : kind * heads + (group + 1) * held] for kind in kinds]
        wide_ref[group, kinds[0] * seq :] = spread(jnp.concatenate(factors, axis=0), one_hot)
    for group in range(groups):
        for tile in range(tiles):
            here = pl.ds(group * per_group + tile * LANES, LANES)
            there = pl.ds(tile * LANES, LANES)
            g = g_ref[:, here].astype(f32)
            v = slope_ref[:, here] * (g * rows_ref[0:1, here] - normed_ref[:, here].astype(f32) * means[group])
            high = v.astype(bf16)
            v_ref[group, 0:seq, there] = high
            if not want_rows:
                v_ref[group, seq : 2 * seq, there] = (v - high.astype(f32)).astype(bf16)
                v_ref[group, 2 * seq :, there] = high
            dy = wide_ref[group, seq : 2 * seq, there] * v
            if dx_ref is not None:
                part_ref[group, :, there] = g + rows_ref[1:2, here] * dy
            if want_rows:
                x = x_ref[:, here].astype(f32)
                found[1].append(jnp.sum(dy * x, axis=0, keepdims=True))
                drive_ref[group, :, there] = (wide_ref[group, 2 * seq :, there] * x).astype(bf16)
        if want_rows:
            q_ref[group] = jnp.dot(scores_ref[group, 1], v_ref[group, 0:seq], preferred_element_type=f32)
            y_ref[group] = jnp.dot(scores_ref[group, 0], drive_ref[group], preferred_element_type=f32)
        else:
            high = scores_ref[group, 1]
            mixer = jnp.concatenate([high, high, scores_ref[group, 2]], axis=1)
            q_ref[group] = jnp.dot(mixer, v_ref[group], preferred_element_type=f32)
    for group in range(groups):
        for tile in range(tiles):
            here = pl.ds(group * per_group + tile * LANES, LANES)
            there = pl.ds(tile * LANES, LANES)
            q = q_ref[group, :, there]
            if dx_ref is not None:
                dx_ref[:, here] = (part_ref[group, :, there] + wide_ref[group, 2 * seq :, there] * q).astype(bf16)
            if want_rows:
                pull = v_ref[group, 0:seq, there].astype(f32) * y_ref[group, :, there] - drive_ref[group, :, there].astype(f32) * q
                found[2].append(jnp.sum(wide_ref[group, 0:seq, there] * pull, axis=0, keepdims=True))
    return [jnp.concatenate(row, axis=1) for row in found] if want_rows else None


def gather_heads(rows, width):
    lane = lax.broadcasted_iota(jnp.int32, (rows.shape[0], LANES), 1)
    sums = jnp.zeros((rows.shape[0], LANES), f32)
    for tile in range(rows.shape[1] // LANES):
        part = rows[:, tile * LANES : (tile + 1) * LANES]
        for side in range(LANES // width):
            mine = jnp.where(lane // width == side, part, 0.0)
            total = jnp.sum(mine, axis=1, keepdims=True)
            sums = jnp.where(lane == tile * (LANES // width) + side, total, sums)
    return sums


def place_rows(found, block, heads, out_ref, earlier_ref):
    gains, skips, logs = found
    share = out_ref.shape[1] - LANES
    parts = gains.shape[1] // share
    for other in range(2):
        row = jnp.where(block == other, gains, 0.0)
        for part in range(parts):
            at = other * parts + part
            piece = row[:, part * share : (part + 1) * share]
            if earlier_ref is not None:
                piece = piece + earlier_ref[at : at + 1, 0:share]
            out_ref[at : at + 1, 0:share] = piece
    sums = gather_heads(jnp.concatenate([skips, logs], axis=0), gains.shape[1] // heads)[:, 0:heads]
    sums = [jnp.where(block == other, sums[kind : kind + 1], 0.0) for kind in range(2) for other in range(2)]
    sums = jnp.concatenate(sums, axis=1)
    if earlier_ref is not None:
        sums = sums + earlier_ref[0:1, share:]
    out_ref[0:1, share:] = sums
    out_ref[1:, share:] = jnp.zeros((out_ref.shape[0] - 1, LANES), f32)


def backward_first(*refs):
    backward(*refs[:7], refs[8:], refs[7], False)


def rows_first(block_ref, *refs):
    heads = refs[5].shape[1] // 3
    place_rows(backward(*refs[:7], refs[8:], None, True), block_ref[0], heads, refs[7], None)


def backward_last(block_ref, earlier_ref, *refs):
    heads = refs[5].shape[1] // 3
    found = backward(*refs[:7], refs[9:], refs[7], True)
    place_rows(found, block_ref[1], heads, refs[8], earlier_ref)


def finish(me_ref, x_ref, gathered_ref, out_ref, alog_ref, dskip_ref, gain_ref, gone):
    parts, _, share = x_ref.shape
    outs = [
        pltpu.make_async_copy(x_ref.at[i], out_ref.at[0, 0, :, pl.ds(i * share, share)], gone.at[i]) for i in range(parts)
    ]
    for copy in outs:
        copy.start()
    me = me_ref[0]
    total = sum(gathered_ref[i] for i in range(gathered_ref.shape[0]))
    lanes = gain_ref.shape[2]
    replicas = total.shape[0] // 2
    held = alog_ref.shape[2]
    for block in range(2):
        row = total[block * replicas : block * replicas + 1, 0:lanes]
        skip, log = [total[0:1, lanes + (kind * 2 + block) * replicas * held :] for kind in range(2)]
        skips, logs = skip[:, 0:held], log[:, 0:held]
        for other in range(1, replicas):
            at = block * replicas + other
            row = jnp.where(me == other, total[at : at + 1, 0:lanes], row)
            skips = jnp.where(me == other, skip[:, other * held : (other + 1) * held], skips)
            logs = jnp.where(me == other, log[:, other * held : (other + 1) * held], logs)
        gain_ref[0, block : block + 1] = row
        dskip_ref[0, block : block + 1] = skips
        alog_ref[0, block : block + 1] = logs
    for copy in outs:
        copy.wait()


def relay_out(x_ref, out_ref, held_ref, came, gone):
    parts, _, share = out_ref.shape
    ins = [
        pltpu.make_async_copy(x_ref.at[0, 0, :, pl.ds(i * share, share)], held_ref.at[i], came.at[i]) for i in range(parts)
    ]
    outs = [pltpu.make_async_copy(held_ref.at[i], out_ref.at[i], gone.at[i]) for i in range(parts)]
    for copy in ins:
        copy.start()
    for first, second in zip(ins, outs):
        first.wait()
        second.start()
    for copy in outs:
        copy.wait()


in_vmem = pl.BlockSpec(memory_space=pltpu.VMEM)
in_smem = pl.BlockSpec(memory_space=pltpu.SMEM)
in_any = pl.BlockSpec(memory_space=pl.ANY)
MIB = 1 << 20


def sized(shape, dtype):
    return jax.ShapeDtypeStruct(tuple(shape), dtype)


def call(kernel, name, in_specs, out_specs, out_shape, scratch=(), grant=16, cost=1):
    return pl.pallas_call(
        kernel,
        in_specs=in_specs,
        out_specs=out_specs,
        out_shape=out_shape,
        scratch_shapes=list(scratch),
        compiler_params=pltpu.CompilerParams(vmem_limit_bytes=grant * MIB),
        cost_estimate=pl.CostEstimate(flops=1000, bytes_accessed=cost * 1000 * 1000, transcendentals=0),
        name=name,
    )


def run_forward(tick, block_table, entry_table, x, z, dt, b, c, alog, dskip, gain):
    seq, chan = x.shape[3:]
    groups = b.shape[4]
    heads = dt.shape[3]
    wide = (groups, seq, chan // groups)
    outs = [
        sized((seq, chan), bf16),
        sized((seq, chan), f32),
        sized((seq, chan), bf16),
        sized((groups, 3, seq, seq), bf16),
        sized((seq, 3 * heads), f32),
        sized((2, chan), f32),
    ]
    scratch = [
        pltpu.VMEM((seq, chan), bf16),
        pltpu.VMEM(dt.shape[3:], f32),
        pltpu.VMEM(b.shape[3:], bf16),
        pltpu.VMEM(c.shape[3:], bf16),
        pltpu.VMEM((groups, 3 * seq, chan // groups), bf16),
    ]
    scratch += [pltpu.VMEM(wide, f32)] * 5 + [pltpu.SemaphoreType.DMA((5,))]
    in_specs = [in_smem] * 2 + [in_any] * 5 + [in_vmem] * 3
    far = [pltpu.with_memory_space_constraint(a, pltpu.HBM) for a in (x, z, dt, b, c)]
    return call(partial(forward, tick), "forward", in_specs, [in_vmem] * 6, outs, scratch, 24, 12)(
        block_table, entry_table, *far, alog, dskip, gain
    )


def backward_scratch(seq, chan, groups):
    wide = (groups, seq, chan // groups)
    tall = (groups, 3 * seq, chan // groups)
    return [pltpu.VMEM(wide, bf16), pltpu.VMEM(tall, bf16)] + [pltpu.VMEM(wide, f32)] * 3 + [pltpu.VMEM(tall, f32)]


def shards(
    grad_in,
    saved_x,
    saved_z,
    saved_dt,
    saved_b,
    saved_c,
    a_log,
    dskip,
    gain,
    block_table,
    entry_table,
):
    parts = lax.axis_size("tensor")
    replicas = lax.axis_size("dp")
    tokens, channels = grad_in.shape[2:]
    share = channels // parts
    seq = tokens * parts
    heads = a_log.shape[2]
    blocks = a_log.shape[1]
    packet = sized((blocks * replicas, share // replicas + LANES), f32)
    block_table = block_table.reshape(-1)
    entry_table = entry_table.reshape(-1)
    steps = jnp.swapaxes(saved_dt, 3, 4)
    me = lax.axis_index("dp").reshape(1)
    staged = call(
        relay_out,
        "relay_out",
        [in_any],
        in_any,
        sized((parts, tokens, share), bf16),
        [pltpu.VMEM((parts, tokens, share), bf16)] + [pltpu.SemaphoreType.DMA((parts,))] * 2,
    )(pltpu.with_memory_space_constraint(grad_in, pltpu.HBM))
    g = lax.all_to_all(staged, "tensor", split_axis=0, concat_axis=0, tiled=True).reshape(seq, share)
    first, last = [
        run_forward(tick, block_table, entry_table, saved_x, saved_z, steps, saved_b, saved_c, a_log, dskip, gain)
        for tick in range(2)
    ]
    scratch = backward_scratch(seq, share, saved_b.shape[4])
    dx = call(backward_first, "backward_first", [in_vmem] * 7, in_vmem, sized((seq, share), bf16), scratch, 20, 6)(g, *first)
    earlier = call(rows_first, "rows_first", [in_smem] + [in_vmem] * 7, in_vmem, packet, scratch, 20, 6)(
        block_table, g, *first
    )
    g = passed_along(dx, "pipe", -1)
    dx, rows = call(
        backward_last,
        "backward_last",
        [in_smem] + [in_vmem] * 8,
        [in_vmem] * 2,
        [sized((seq, share), bf16), packet],
        scratch,
        20,
        6,
    )(block_table, earlier, g, *last)
    out = lax.all_to_all(dx.reshape(parts, tokens, share), "tensor", split_axis=0, concat_axis=0, tiled=True)
    rows = lax.all_gather(rows, "dp")
    out, grad_alog, grad_dskip, grad_gain = call(
        finish,
        "finish",
        [in_smem] + [in_vmem] * 2,
        [in_any] + [in_vmem] * 3,
        [
            sized(grad_in.shape, bf16),
            sized((1, blocks, heads // replicas), f32),
            sized((1, blocks, heads // replicas), f32),
            sized((1, blocks, share // replicas), f32),
        ],
        [pltpu.SemaphoreType.DMA((parts,))],
    )(me, out, rows)
    return (out, grad_alog, grad_dskip, grad_gain)


def solution(mesh):
    placed = (
        P("pipe", "dp", "tensor", None),
        P("pipe", "dp", None, None, "tensor"),
        P("pipe", "dp", None, None, "tensor"),
        P("pipe", "dp", None, None, "tensor"),
        P("pipe", "dp", None, None, "tensor", None),
        P("pipe", "dp", None, None, "tensor", None),
        P("pipe", None, "tensor"),
        P("pipe", None, "tensor"),
        P("pipe", None, "tensor"),
        P(None, "pipe", "dp"),
        P(None, "pipe", "dp"),
    )
    return jax.shard_map(
        shards,
        mesh=mesh,
        in_specs=placed,
        out_specs=(
            P("pipe", "dp", "tensor", None),
            P("pipe", None, ("tensor", "dp")),
            P("pipe", None, ("tensor", "dp")),
            P("pipe", None, ("tensor", "dp")),
        ),
        check_vma=False,
    )
```

profile of v0, /device:TPU:1, one launch (start us, length us, event | category | flops | bytes accessed | tf_op | source)
XLA Modules:
  0.0 56.0 jit_solution(16165269947521969934)
XLA Ops:
  0.6 0.0 copy-start.1
  0.6 0.0 copy-start.4
  0.7 0.0 copy-start.2
  0.7 0.0 copy-start.3
  0.7 0.0 copy-start
  0.7 1.8 %relay_out.1 = bf16[4,32,2048]{2,1,0:T(8,128)(2,1)} custom-call(bf16[1,1,32,8192]{3,2,1,0:T(8,128)(2,1)} %x_ref.1), custom_call_target="tpu_custom_call" | custom-call | flops 1000 | bytes 1000000 | tf_op jit(solution)/shard_map/relay_out/pallas_call | solution.py:404
  2.5 5.0 %all-to-all-start = ((bf16[4,32,2048]{2,1,0:T(8,128)(2,1)}), bf16[4,32,2048]{2,1,0:T(8,128)(2,1)S(1)}, u32[]{:S(2)}, u32[]{:S(2)}) async-start(bf16[4,32,2048]{2,1,0:T(8,128)(2,1)} %relay_out.1), calls=%async_computation | async-start | bytes 1048576 | tf_op jit(solution)/shard_map/all_to_all | solution.py:412
  7.6 0.0 copy-done.1
  7.6 0.0 copy-done.4
  7.6 0.0 copy-done.2
  7.6 0.0 copy-done.3
  7.6 0.0 copy-done
  7.6 3.9 %forward.2 = (bf16[128,2048]{1,0:T(8,128)(2,1)S(1)}, f32[128,2048]{1,0:T(8,128)S(1)}, bf16[128,2048]{1,0:T(8,128)(2,1)S(1)}, bf16[2,3,128,128]{3,2,1,0:T(8,128)(...) custom-call(s32[2]{0:T(128)S(1)} %bitcast.10, s32[2]{0:T(128)S(1)} %bitcast.14, ...), custom_call_target="tpu_custom_call" | custom-call | flops 1000 | bytes 12000000 | tf_op jit(solution)/shard_map/forward/pallas_call | solution.py:368
  11.5 3.0 %all-to-all-done = bf16[4,32,2048]{2,1,0:T(8,128)(2,1)S(1)} async-done(((bf16[4,32,2048]{2,1,0:T(8,128)(2,1)}), bf16[4,32,2048]{2,1,0:T(8,128)(2,1)S(1)}, u32[]{:S(2)}, u32[]{:S(2)}) %all-to-all-start) | async-done | bytes 524320 | tf_op jit(solution)/shard_map/all_to_all | solution.py:412
  14.5 1.3 %backward_first.1 = bf16[128,2048]{1,0:T(8,128)(2,1)S(1)} custom-call(bf16[128,2048]{1,0:T(8,128)(2,1)S(1)} %bitcast.7, bf16[128,2048]{1,0:T(8,128)(2,1)S(1)} %get-tuple-element.18.refs_1_, f32[128,2048]{1,0:T(8,128)S(1)} %get-tuple-element.19.refs_2_, bf16[128,2048]{1,0:T(8,128)(2,1)S(1)} %get-tuple-element.20.refs_3_, ...), custom_call_target="tpu_custom_call" | custom-call | flops 1000 | bytes 6000000 | tf_op jit(solution)/shard_map/backward_first/pallas_call | solution.py:418
  15.8 13.4 %collective-permute-start = (bf16[128,2048]{1,0:T(8,128)(2,1)S(1)}, bf16[128,2048]{1,0:T(8,128)(2,1)S(1)}, u32[]{:S(2)}, u32[]{:S(2)}) collective-permute-start(bf16[128,2048]{1,0:T(8,128)(2,1)S(1)} %backward_first.1), channel_id=1, source_target_pairs={{16,0},{32,16},{48,32},{64,48},{80,64},{96,80},{112,96},{128,112},... | collective-permute-start | bytes 1572872 | tf_op jit(solution)/shard_map/ppermute | solution.py:19
  29.2 3.9 %forward.3 = (bf16[128,2048]{1,0:T(8,128)(2,1)S(1)}, f32[128,2048]{1,0:T(8,128)S(1)}, bf16[128,2048]{1,0:T(8,128)(2,1)S(1)}, bf16[2,3,128,128]{3,2,1,0:T(8,128)(...) custom-call(s32[2]{0:T(128)S(1)} %bitcast.11, s32[2]{0:T(128)S(1)} %bitcast.15, ...), custom_call_target="tpu_custom_call" | custom-call | flops 1000 | bytes 12000000 | tf_op jit(solution)/shard_map/forward/pallas_call | solution.py:368
  33.1 2.2 %rows_first.1.earlier_ref = f32[8,640]{1,0:T(8,128)S(1)} custom-call(s32[2]{0:T(128)S(1)} %bitcast.12, bf16[128,2048]{1,0:T(8,128)(2,1)S(1)} %bitcast.8, bf16[128,2048]{1,0:T(8,128)(2,1)S(1)} %get-tuple-element.18.refs_1_, f32[128,2048]{1,0:T(8,128)S(1)} %get-tuple-element.19.refs_2_, bf16[128,2048]{1,0:T(8,128)(2,1)S(1)} %get-tuple-element.20.refs_3_, ...), custom_call_target="tpu_custom_call" | custom-call | flops 1000 | bytes 6000000 | tf_op jit(solution)/shard_map/rows_first/pallas_call | solution.py:419
  35.3 2.9 %collective-permute-done.refs_0_ = bf16[128,2048]{1,0:T(8,128)(2,1)S(1)} collective-permute-done((bf16[128,2048]{1,0:T(8,128)(2,1)S(1)}, bf16[128,2048]{1,0:T(8,128)(2,1)S(1)}, u32[]{:S(2)}, u32[]{:S(2)}) %collective-permute-start) | collective-permute-done | bytes 524320 | tf_op jit(solution)/shard_map/ppermute | solution.py:19
  38.3 3.0 %backward_last.1 = (bf16[128,2048]{1,0:T(8,128)(2,1)}, f32[8,640]{1,0:T(8,128)S(1)}) custom-call(s32[2]{0:T(128)S(1)} %bitcast.13, f32[8,640]{1,0:T(8,128)S(1)} %rows_first.1.earlier_ref, bf16[128,2048]{1,0:T(8,128)(2,1)S(1)} %collective-permute-done.refs_0_, bf16[128,2048]{1,0:T(8,128)(2,1)S(1)} %get-tuple-element.24.refs_1_, ...), custom_call_target="tpu_custom_call" | custom-call | flops 1000 | bytes 6000000 | tf_op jit(solution)/shard_map/backward_last/pallas_call | solution.py:423
  41.3 3.5 %all-to-all-start.1 = ((bf16[4,32,2048]{2,1,0:T(8,128)(2,1)}), bf16[4,32,2048]{2,1,0:T(8,128)(2,1)S(1)}, u32[]{:S(2)}, u32[]{:S(2)}) async-start(bf16[4,32,2048]{2,1,0:T(8,128)(2,1)} %bitcast.5), calls=%async_computation.1 | async-start | bytes 1048576 | tf_op jit(solution)/shard_map/all_to_all | solution.py:433
  44.8 9.7 %all-gather = f32[32,640]{1,0:T(8,128)S(1)} all-gather(f32[8,640]{1,0:T(8,128)S(1)} %get-tuple-element.31), channel_id=2, replica_groups=mesh['pipe'=32,'tensor'=4,'dp'=4] {'dp'}, dimensions={0}, use_global_device_ids=true | all-gather | bytes 102400 | tf_op jit(solution)/shard_map/all_gather | solution.py:434
  54.5 0.0 all-to-all-done.1.x_ref
  54.5 1.5 %finish.1 = (bf16[1,1,32,8192]{3,2,1,0:T(8,128)(2,1)}, f32[1,2,8]{2,1,0:T(2,128)}, f32[1,2,8]{2,1,0:T(2,128)}, f32[1,2,512]{2,1,0:T(2,128)}) custom-call(s32[1]{0:T(128)} %bitcast.me_ref, bf16[4,32,2048]{2,1,0:T(8,128)(2,1)S(1)} %all-to-all-done.1.x_ref, f32[4,8,640]{2,1,0:T(8,128)S(1)} %bitcast.9), custom_call_target="tpu_custom_call" | custom-call | flops 1000 | bytes 1000000 | tf_op jit(solution)/shard_map/finish/pallas_call | solution.py:435
Async XLA Ops:
  0.6 6.9 %copy-start.1 = (s32[2,1,1]{0,2,1:T(1,128)S(1)}, s32[2,1,1]{0,2,1:T(1,128)}, u32[]{:S(2)}) copy-start(s32[2,1,1]{0,2,1:T(1,128)} %param.20) | copy-start | bytes 28
  0.6 6.9 %copy-start.4 = (s32[2,1,1]{0,2,1:T(1,128)S(1)}, s32[2,1,1]{0,2,1:T(1,128)}, u32[]{:S(2)}) copy-start(s32[2,1,1]{0,2,1:T(1,128)} %param.21) | copy-start | bytes 28
  0.7 6.9 %copy-start.2 = (f32[1,2,32]{2,1,0:T(2,128)S(1)}, f32[1,2,32]{2,1,0:T(2,128)}, u32[]{:S(2)}) copy-start(f32[1,2,32]{2,1,0:T(2,128)} %alog_ref.3) | copy-start | bytes 772
  0.7 6.9 %copy-start.3 = (f32[1,2,32]{2,1,0:T(2,128)S(1)}, f32[1,2,32]{2,1,0:T(2,128)}, u32[]{:S(2)}) copy-start(f32[1,2,32]{2,1,0:T(2,128)} %dskip_ref.3) | copy-start | bytes 772
  0.7 6.9 %copy-start = (f32[1,2,2048]{2,1,0:T(2,128)S(1)}, f32[1,2,2048]{2,1,0:T(2,128)}, u32[]{:S(2)}) copy-start(f32[1,2,2048]{2,1,0:T(2,128)} %gain_ref.3) | copy-start | bytes 49156
  2.5 12.0 %all-to-all-start = ((bf16[4,32,2048]{2,1,0:T(8,128)(2,1)}), bf16[4,32,2048]{2,1,0:T(8,128)(2,1)S(1)}, u32[]{:S(2)}, u32[]{:S(2)}) async-start(bf16[4,32,2048]{2,1,0:T(8,128)(2,1)} %relay_out.1), calls=%async_computation | async-start | bytes 1048576 | tf_op jit(solution)/shard_map/all_to_all | solution.py:412
  15.8 22.4 %collective-permute-start = (bf16[128,2048]{1,0:T(8,128)(2,1)S(1)}, bf16[128,2048]{1,0:T(8,128)(2,1)S(1)}, u32[]{:S(2)}, u32[]{:S(2)}) collective-permute-start(bf16[128,2048]{1,0:T(8,128)(2,1)S(1)} %backward_first.1), channel_id=1, source_target_pairs={{16,0},{32,16},{48,32},{64,48},{80,64},{96,80},{112,96},{128,112},... | collective-permute-start | bytes 1572872 | tf_op jit(solution)/shard_map/ppermute | solution.py:19
  41.3 13.2 %all-to-all-start.1 = ((bf16[4,32,2048]{2,1,0:T(8,128)(2,1)}), bf16[4,32,2048]{2,1,0:T(8,128)(2,1)S(1)}, u32[]{:S(2)}, u32[]{:S(2)}) async-start(bf16[4,32,2048]{2,1,0:T(8,128)(2,1)} %bitcast.5), calls=%async_computation.1 | async-start | bytes 1048576 | tf_op jit(solution)/shard_map/all_to_all | solution.py:433
where the time goes:
time: 56.4 us; the launch traced here: 56 us
  starting transfers between devices  21.9 us (39%)
  Pallas kernels  17.7 us (31%)
  blocking collectives  9.71 us (17%)
  waiting for transfers between devices  5.91 us (10%)
  between operations  0.75 us (1%)
    ppermute x1, starting transfers between devices, passed_along(): return lax.ppermute(block, axis, route)  13.4 us
    all_gather x1, blocking collectives, shards(): rows = lax.all_gather(rows, 'dp')  9.71 us
    pallas_call x2, Pallas kernels, run_forward(): call(partial(forward, tick), 'forward', in_specs, [in_vmem] * 6, outs, sc...  7.81 us
    all_to_all x1, starting transfers between devices, shards(): lax.all_to_all(staged, 'tensor', split_axis=0, concat_axis=0, tiled=True)  5.02 us
    all_to_all x1, starting transfers between devices, shards(): lax.all_to_all(dx.reshape(parts, tokens, share), 'tensor', split_axis=0,...  3.47 us
    pallas_call x1, Pallas kernels, shards(): call(backward_last, 'backward_last', [in_smem] + [in_vmem] * 8, [in_vmem]...  3.04 us
    all_to_all x1, waiting for transfers between devices, shards(): lax.all_to_all(staged, 'tensor', split_axis=0, concat_axis=0, tiled=True)  2.99 us
    ppermute x1, waiting for transfers between devices, passed_along(): return lax.ppermute(block, axis, route)  2.92 us
  transfers between devices with their start and end apart: 3, of which 2 were waited for; matrix products, arithmetic and copies ran while one was open for 0% of the time, Pallas kernels for 18%

commit v1 on v0

--- a/solution.py
+++ b/solution.py
@@ -11,6 +11,7 @@
 f32 = jnp.float32
 bf16 = jnp.bfloat16
 LANES = 128
+WIDTH = 64
 
 
 def passed_along(block, axis, distance):
@@ -35,9 +36,10 @@
 
 
 def spread_map(heads, width):
-    head = lax.broadcasted_iota(jnp.int32, (3 * heads, heads * width), 0) % heads
-    lane = lax.broadcasted_iota(jnp.int32, (3 * heads, heads * width), 1)
-    return (lane // width == head).astype(bf16)
+    first = lax.broadcasted_iota(jnp.int32, (heads, heads * width), 0) * width
+    lane = lax.broadcasted_iota(jnp.int32, (heads, heads * width), 1)
+    one_hot = jnp.where((lane >= first) & (lane < first + width), 1.0, 0.0).astype(bf16)
+    return jnp.concatenate([one_hot] * 3, axis=0)
 
 
 def spread(values, one_hot):
@@ -61,24 +63,17 @@
     alog_ref,
     dskip_ref,
     gain_ref,
-    x_ref,
     slope_ref,
     normed_ref,
     scores_ref,
-    heads_ref,
     rows_ref,
-    z_ref,
-    dt_ref,
-    b_ref,
-    c_ref,
-    drive_ref,
-    wx_ref,
-    ec_ref,
-    y_ref,
-    gated_ref,
-    gate_ref,
-    sem,
+    *refs,
 ):
+    if tick:
+        wx_out, skips_ref, moved_ref, mixed_ref, driven_ref, wide_ref, x_ref, *refs = refs
+    else:
+        x_ref, heads_ref, *refs = refs
+    z_ref, dt_ref, b_ref, c_ref, drive_ref, wx_ref, ec_ref, y_ref, gated_ref, gate_ref, sem = refs
     block = block_ref[tick]
     entry = entry_ref[tick]
     moves = [
@@ -115,14 +110,17 @@
     grow = jnp.exp(-cum)
     fall = jnp.exp(cum)
     weight = grow * steps[seq:]
-    heads_ref[:, 0:heads] = cum
-    heads_ref[:, heads : 2 * heads] = grow
-    heads_ref[:, 2 * heads : 3 * heads] = weight
+    if not tick:
+        heads_ref[:, 0:heads] = cum
+        heads_ref[:, heads : 2 * heads] = grow
+        heads_ref[:, 2 * heads : 3 * heads] = weight
     for group in range(groups):
         mine = slice(group * held, (group + 1) * held)
         both = spread(jnp.concatenate([weight[:, mine], fall[:, mine]], axis=0), one_hot)
         wx_ref[group] = both[0:seq]
         ec_ref[group] = both[seq:]
+        if tick:
+            wide_ref[group] = spread(jnp.concatenate([grow[:, mine], cum[:, mine]], axis=0), one_hot)
     moves[1].wait()
     moves[2].wait()
     mixers = []
@@ -140,10 +138,24 @@
         for tile in range(tiles):
             here = pl.ds(group * per_group + tile * LANES, LANES)
             there = pl.ds(tile * LANES, LANES)
-            high, low = halves(wx_ref[group, :, there] * x_ref[:, here].astype(f32))
+            x = x_ref[:, here].astype(f32)
+            wx = wx_ref[group, :, there]
+            high, low = halves(wx * x)
+            if tick:
+                wx_out[:, here] = wx
+                grown = wide_ref[group, 0:seq, there]
+                skips_ref[:, here] = grown * rows_ref[1:2, here]
+                moved_ref[:, here] = grown * x
+                driven_ref[:, here] = wide_ref[group, seq:, there] * high.astype(f32)
             drive_ref[group, 0:seq, there] = high
             drive_ref[group, seq : 2 * seq, there] = low
             drive_ref[group, 2 * seq :, there] = high
+        if tick:
+            y_ref[group] = jnp.dot(scores_ref[group, 0], drive_ref[group, 0:seq], preferred_element_type=f32)
+            for tile in range(tiles):
+                here = pl.ds(group * per_group + tile * LANES, LANES)
+                there = pl.ds(tile * LANES, LANES)
+                mixed_ref[:, here] = wide_ref[group, seq:, there] * y_ref[group, :, there]
         y_ref[group] = jnp.dot(mixers[group], drive_ref[group], preferred_element_type=f32)
     moves[4].wait()
     for group in range(groups):
@@ -166,7 +178,7 @@
             slope_ref[:, here] = gate_ref[group, :, there] * scale
 
 
-def backward(g_ref, x_ref, slope_ref, normed_ref, scores_ref, heads_ref, rows_ref, scratch, dx_ref, want_rows):
+def backward(g_ref, slope_ref, normed_ref, scores_ref, rows_ref, x_ref, heads_ref, scratch, dx_ref, want_rows):
     drive_ref, v_ref, q_ref, y_ref, part_ref, wide_ref = scratch
     seq, chan = normed_ref.shape
     groups = scores_ref.shape[0]
@@ -228,37 +240,35 @@
     return [jnp.concatenate(row, axis=1) for row in found] if want_rows else None
 
 
-def gather_heads(rows, width):
-    lane = lax.broadcasted_iota(jnp.int32, (rows.shape[0], LANES), 1)
-    sums = jnp.zeros((rows.shape[0], LANES), f32)
-    for tile in range(rows.shape[1] // LANES):
-        part = rows[:, tile * LANES : (tile + 1) * LANES]
-        for side in range(LANES // width):
-            mine = jnp.where(lane // width == side, part, 0.0)
-            total = jnp.sum(mine, axis=1, keepdims=True)
-            sums = jnp.where(lane == tile * (LANES // width) + side, total, sums)
-    return sums
-
-
 def place_rows(found, block, heads, out_ref, earlier_ref):
     gains, skips, logs = found
+    height = out_ref.shape[0]
     share = out_ref.shape[1] - LANES
     parts = gains.shape[1] // share
-    for other in range(2):
-        row = jnp.where(block == other, gains, 0.0)
-        for part in range(parts):
-            at = other * parts + part
-            piece = row[:, part * share : (part + 1) * share]
-            if earlier_ref is not None:
-                piece = piece + earlier_ref[at : at + 1, 0:share]
-            out_ref[at : at + 1, 0:share] = piece
-    sums = gather_heads(jnp.concatenate([skips, logs], axis=0), gains.shape[1] // heads)[:, 0:heads]
-    sums = [jnp.where(block == other, sums[kind : kind + 1], 0.0) for kind in range(2) for other in range(2)]
-    sums = jnp.concatenate(sums, axis=1)
+    width = gains.shape[1] // heads
+    row = lax.broadcasted_iota(jnp.int32, (height, share), 0) - block * parts
+    mine = jnp.zeros((height, share), f32)
+    for part in range(parts):
+        piece = jnp.broadcast_to(gains[:, part * share : (part + 1) * share], (height, share))
+        mine = jnp.where(row == part, piece, mine)
+    lane = lax.broadcasted_iota(jnp.int32, (1, LANES), 1)
+    sums = jnp.zeros((1, LANES), f32)
+    for tile in range(gains.shape[1] // LANES):
+        here = slice(tile * LANES, (tile + 1) * LANES)
+        for kind, rows in enumerate((skips, logs)):
+            whole = rows[:, here]
+            for side in range(LANES // width):
+                inside = (lane >= side * width) & (lane < (side + 1) * width)
+                total = jnp.sum(jnp.where(inside, whole, 0.0), axis=1, keepdims=True)
+                head = tile * (LANES // width) + side
+                sums = jnp.where(lane == (2 * kind + block) * heads + head, total, sums)
+    top = lax.broadcasted_iota(jnp.int32, (height, LANES), 0) == 0
+    sums = jnp.where(top, jnp.broadcast_to(sums, (height, LANES)), 0.0)
     if earlier_ref is not None:
-        sums = sums + earlier_ref[0:1, share:]
-    out_ref[0:1, share:] = sums
-    out_ref[1:, share:] = jnp.zeros((out_ref.shape[0] - 1, LANES), f32)
+        mine = mine + earlier_ref[:, 0:share]
+        sums = sums + earlier_ref[:, share:]
+    out_ref[:, 0:share] = mine
+    out_ref[:, share:] = sums
 
 
 def backward_first(*refs):
@@ -266,23 +276,78 @@
 
 
 def rows_first(block_ref, *refs):
-    heads = refs[5].shape[1] // 3
+    heads = refs[6].shape[1] // 3
     place_rows(backward(*refs[:7], refs[8:], None, True), block_ref[0], heads, refs[7], None)
 
 
-def backward_last(block_ref, earlier_ref, *refs):
-    heads = refs[5].shape[1] // 3
-    found = backward(*refs[:7], refs[9:], refs[7], True)
-    place_rows(found, block_ref[1], heads, refs[8], earlier_ref)
-
-
-def finish(me_ref, x_ref, gathered_ref, out_ref, alog_ref, dskip_ref, gain_ref, gone):
+def backward_last(
+    block_ref,
+    earlier_ref,
+    g_ref,
+    slope_ref,
+    normed_ref,
+    scores_ref,
+    gain_ref,
+    wx_ref,
+    skips_ref,
+    moved_ref,
+    mixed_ref,
+    driven_ref,
+    out_ref,
+    packet_ref,
+    dx_ref,
+    v_ref,
+    q_ref,
+    part_ref,
+    sem,
+):
+    seq, chan = normed_ref.shape
+    groups = scores_ref.shape[0]
+    per_group = chan // groups
+    tiles = per_group // LANES
+    found = [[], [], []]
+    moves = []
+    for group in range(groups):
+        total = jnp.zeros((seq, LANES), f32)
+        for tile in range(tiles):
+            here = pl.ds(group * per_group + tile * LANES, LANES)
+            gn = g_ref[:, here].astype(f32) * normed_ref[:, here].astype(f32)
+            total = total + gn * gain_ref[0:1, here]
+            found[0].append(jnp.sum(gn, axis=0, keepdims=True))
+        mean = jnp.sum(total, axis=1, keepdims=True) * (1.0 / per_group)
+        for tile in range(tiles):
+            here = pl.ds(group * per_group + tile * LANES, LANES)
+            there = pl.ds(tile * LANES, LANES)
+            g = g_ref[:, here].astype(f32)
+            v = slope_ref[:, here] * (g * gain_ref[0:1, here] - normed_ref[:, here].astype(f32) * mean)
+            v_ref[group, :, there] = v.astype(bf16)
+            part_ref[group, :, there] = g + skips_ref[:, here] * v
+            found[1].append(jnp.sum(moved_ref[:, here] * v, axis=0, keepdims=True))
+        q_ref[group] = jnp.dot(scores_ref[group, 1], v_ref[group], preferred_element_type=f32)
+    for group in range(groups):
+        for tile in range(tiles):
+            here = pl.ds(group * per_group + tile * LANES, LANES)
+            there = pl.ds(tile * LANES, LANES)
+            q = q_ref[group, :, there]
+            dx_ref[:, here] = (part_ref[group, :, there] + wx_ref[:, here] * q).astype(bf16)
+            pull = v_ref[group, :, there].astype(f32) * mixed_ref[:, here] - driven_ref[:, here] * q
+            found[2].append(jnp.sum(pull, axis=0, keepdims=True))
+        here = pl.ds(group * per_group, per_group)
+        moves.append(pltpu.make_async_copy(dx_ref.at[:, here], out_ref.at[:, here], sem.at[group]))
+        moves[-1].start()
+    rows = [jnp.concatenate(row, axis=1) for row in found]
+    place_rows(rows, block_ref[1], chan // WIDTH, packet_ref, earlier_ref)
+    for move in moves:
+        move.wait()
+
+
+def finish(me_ref, x_ref, gathered_ref, out_ref, alog_out, dskip_out, gain_out, alog_ref, dskip_ref, gain_ref, sem):
     parts, _, share = x_ref.shape
-    outs = [
-        pltpu.make_async_copy(x_ref.at[i], out_ref.at[0, 0, :, pl.ds(i * share, share)], gone.at[i]) for i in range(parts)
+    moves = [
+        pltpu.make_async_copy(x_ref.at[i], out_ref.at[0, 0, :, pl.ds(i * share, share)], sem.at[i]) for i in range(parts)
     ]
-    for copy in outs:
-        copy.start()
+    for move in moves:
+        move.start()
     me = me_ref[0]
     total = sum(gathered_ref[i] for i in range(gathered_ref.shape[0]))
     lanes = gain_ref.shape[2]
@@ -300,8 +365,11 @@
         gain_ref[0, block : block + 1] = row
         dskip_ref[0, block : block + 1] = skips
         alog_ref[0, block : block + 1] = logs
-    for copy in outs:
-        copy.wait()
+    for i, (src, dst) in enumerate(((alog_ref, alog_out), (dskip_ref, dskip_out), (gain_ref, gain_out))):
+        moves.append(pltpu.make_async_copy(src, dst, sem.at[parts + i]))
+        moves[-1].start()
+    for move in moves:
+        move.wait()
 
 
 def relay_out(x_ref, out_ref, held_ref, came, gone):
@@ -347,15 +415,15 @@
     groups = b.shape[4]
     heads = dt.shape[3]
     wide = (groups, seq, chan // groups)
-    outs = [
-        sized((seq, chan), bf16),
-        sized((seq, chan), f32),
-        sized((seq, chan), bf16),
-        sized((groups, 3, seq, seq), bf16),
-        sized((seq, 3 * heads), f32),
-        sized((2, chan), f32),
-    ]
-    scratch = [
+    flat = sized((seq, chan), f32)
+    outs = [flat, sized((seq, chan), bf16), sized((groups, 3, seq, seq), bf16), sized((2, chan), f32)]
+    if tick:
+        outs += [flat] * 5
+        scratch = [pltpu.VMEM((groups, 2 * seq, chan // groups), f32), pltpu.VMEM((seq, chan), bf16)]
+    else:
+        outs += [sized((seq, chan), bf16), sized((seq, 3 * heads), f32)]
+        scratch = []
+    scratch += [
         pltpu.VMEM((seq, chan), bf16),
         pltpu.VMEM(dt.shape[3:], f32),
         pltpu.VMEM(b.shape[3:], bf16),
@@ -365,7 +433,7 @@
     scratch += [pltpu.VMEM(wide, f32)] * 5 + [pltpu.SemaphoreType.DMA((5,))]
     in_specs = [in_smem] * 2 + [in_any] * 5 + [in_vmem] * 3
     far = [pltpu.with_memory_space_constraint(a, pltpu.HBM) for a in (x, z, dt, b, c)]
-    return call(partial(forward, tick), "forward", in_specs, [in_vmem] * 6, outs, scratch, 24, 12)(
+    return call(partial(forward, tick), "forward", in_specs, [in_vmem] * len(outs), outs, scratch, 24, 12)(
         block_table, entry_table, *far, alog, dskip, gain
     )
 
@@ -423,27 +491,23 @@
     dx, rows = call(
         backward_last,
         "backward_last",
-        [in_smem] + [in_vmem] * 8,
-        [in_vmem] * 2,
-        [sized((seq, share), bf16), packet],
-        scratch,
+        [in_smem] + [in_vmem] * 11,
+        [in_any, in_vmem],
+        [pltpu.HBM((seq, share), bf16), packet],
+        [pltpu.VMEM((seq, share), bf16), scratch[0], *scratch[2:4], pltpu.SemaphoreType.DMA((saved_b.shape[4],))],
         20,
         6,
     )(block_table, earlier, g, *last)
     out = lax.all_to_all(dx.reshape(parts, tokens, share), "tensor", split_axis=0, concat_axis=0, tiled=True)
     rows = lax.all_gather(rows, "dp")
+    shapes = [(1, blocks, heads // replicas)] * 2 + [(1, blocks, share // replicas)]
     out, grad_alog, grad_dskip, grad_gain = call(
         finish,
         "finish",
         [in_smem] + [in_vmem] * 2,
-        [in_any] + [in_vmem] * 3,
-        [
-            sized(grad_in.shape, bf16),
-            sized((1, blocks, heads // replicas), f32),
-            sized((1, blocks, heads // replicas), f32),
-            sized((1, blocks, share // replicas), f32),
-        ],
-        [pltpu.SemaphoreType.DMA((parts,))],
+        [in_any] * 4,
+        [sized(grad_in.shape, bf16)] + [sized(shape, f32) for shape in shapes],
+        [pltpu.VMEM(shape, f32) for shape in shapes] + [pltpu.SemaphoreType.DMA((parts + 3,))],
     )(me, out, rows)
     return (out, grad_alog, grad_dskip, grad_gain)
 

time: 56.4 us -> 55.4 us (0.982)
  waiting for transfers between devices: 5.91 us -> 5.26 us
    ppermute x1, waiting for transfers between devices: 2.92 us -> 2.28 us  [passed_along(): return lax.ppermute(block, axis, route)]
  transfers between devices with their start and end apart: 3 -> 3, of which waited for: 2 -> 2; matrix products, arithmetic and copies ran while one was open for 0% -> 0% of each run, Pallas kernels for 18% -> 19%
where the time goes in v1:
time: 55.4 us; the launch traced here: 55 us
  starting transfers between devices  21.9 us (40%)
  Pallas kernels  17.3 us (31%)
  blocking collectives  9.7 us (18%)
  waiting for transfers between devices  5.26 us (9%)
  between operations  0.76 us (1%)
    ppermute x1, starting transfers between devices, passed_along(): return lax.ppermute(block, axis, route)  13.4 us
    all_gather x1, blocking collectives, shards(): rows = lax.all_gather(rows, 'dp')  9.7 us
    pallas_call x2, Pallas kernels, run_forward(): call(partial(forward, tick), 'forward', in_specs, [in_vmem] * len(outs),...  8.5 us
    all_to_all x1, starting transfers between devices, shards(): lax.all_to_all(staged, 'tensor', split_axis=0, concat_axis=0, tiled=True)  5.02 us
    all_to_all x1, starting transfers between devices, shards(): lax.all_to_all(dx.reshape(parts, tokens, share), 'tensor', split_axis=0,...  3.48 us
    all_to_all x1, waiting for transfers between devices, shards(): lax.all_to_all(staged, 'tensor', split_axis=0, concat_axis=0, tiled=True)  2.98 us
    pallas_call x1, Pallas kernels, shards(): call(backward_last, 'backward_last', [in_smem] + [in_vmem] * 11, [in_any,...  2.55 us
    ppermute x1, waiting for transfers between devices, passed_along(): return lax.ppermute(block, axis, route)  2.28 us
  transfers between devices with their start and end apart: 3, of which 2 were waited for; matrix products, arithmetic and copies ran while one was open for 0% of the time, Pallas kernels for 19%

profile of v1, /device:TPU:1, one launch (start us, length us, event | category | flops | bytes accessed | tf_op | source)
XLA Modules:
  0.0 55.0 jit_solution(3280064038926942619)
XLA Ops:
  0.6 0.0 copy-start.1
  0.6 0.0 copy-start.4
  0.7 0.0 copy-start.2
  0.7 0.0 copy-start.3
  0.7 0.0 copy-start
  0.7 1.8 %relay_out.1 = bf16[4,32,2048]{2,1,0:T(8,128)(2,1)} custom-call(bf16[1,1,32,8192]{3,2,1,0:T(8,128)(2,1)} %x_ref.1), custom_call_target="tpu_custom_call" | custom-call | flops 1000 | bytes 1000000 | tf_op jit(solution)/shard_map/relay_out/pallas_call | solution.py:472
  2.5 5.0 %all-to-all-start = ((bf16[4,32,2048]{2,1,0:T(8,128)(2,1)}), bf16[4,32,2048]{2,1,0:T(8,128)(2,1)S(1)}, u32[]{:S(2)}, u32[]{:S(2)}) async-start(bf16[4,32,2048]{2,1,0:T(8,128)(2,1)} %relay_out.1), calls=%async_computation | async-start | bytes 1048576 | tf_op jit(solution)/shard_map/all_to_all | solution.py:480
  7.6 0.0 copy-done.1
  7.6 0.0 copy-done.4
  7.6 0.0 copy-done.2
  7.6 0.0 copy-done.3
  7.6 0.0 copy-done
  7.6 3.9 %forward.2 = (f32[128,2048]{1,0:T(8,128)S(1)}, bf16[128,2048]{1,0:T(8,128)(2,1)S(1)}, bf16[2,3,128,128]{3,2,1,0:T(8,128)(2,1)S(1)}, f32[2,2048]{1,0:T(2,128)S(1)...) custom-call(s32[2]{0:T(128)S(1)} %bitcast.10, s32[2]{0:T(128)S(1)} %bitcast.14, ...), custom_call_target="tpu_custom_call" | custom-call | flops 1000 | bytes 12000000 | tf_op jit(solution)/shard_map/forward/pallas_call | solution.py:436
  11.5 3.0 %all-to-all-done = bf16[4,32,2048]{2,1,0:T(8,128)(2,1)S(1)} async-done(((bf16[4,32,2048]{2,1,0:T(8,128)(2,1)}), bf16[4,32,2048]{2,1,0:T(8,128)(2,1)S(1)}, u32[]{:S(2)}, u32[]{:S(2)}) %all-to-all-start) | async-done | bytes 524320 | tf_op jit(solution)/shard_map/all_to_all | solution.py:480
  14.5 1.3 %backward_first.1 = bf16[128,2048]{1,0:T(8,128)(2,1)S(1)} custom-call(bf16[128,2048]{1,0:T(8,128)(2,1)S(1)} %bitcast.7, f32[128,2048]{1,0:T(8,128)S(1)} %get-tuple-element.21.refs_1_, bf16[128,2048]{1,0:T(8,128)(2,1)S(1)} %get-tuple-element.22.refs_2_, bf16[2,3,128,128]{3,2,1,0:T(8,128)(2,1)S(1)} %get-tuple-element.23.refs_3_, ...), custom_call_target="tpu_custom_call" | custom-call | flops 1000 | bytes 6000000 | tf_op jit(solution)/shard_map/backward_first/pallas_call | solution.py:486
  15.8 13.4 %collective-permute-start = (bf16[128,2048]{1,0:T(8,128)(2,1)S(1)}, bf16[128,2048]{1,0:T(8,128)(2,1)S(1)}, u32[]{:S(2)}, u32[]{:S(2)}) collective-permute-start(bf16[128,2048]{1,0:T(8,128)(2,1)S(1)} %backward_first.1), channel_id=1, source_target_pairs={{16,0},{32,16},{48,32},{64,48},{80,64},{96,80},{112,96},{128,112},... | collective-permute-start | bytes 1572872 | tf_op jit(solution)/shard_map/ppermute | solution.py:20
  29.2 4.6 %forward.3 = (f32[128,2048]{1,0:T(8,128)S(1)}, bf16[128,2048]{1,0:T(8,128)(2,1)S(1)}, bf16[2,3,128,128]{3,2,1,0:T(8,128)(2,1)S(1)}, f32[2,2048]{1,0:T(2,128)S(1)...) custom-call(s32[2]{0:T(128)S(1)} %bitcast.11, ...), custom_call_target="tpu_custom_call" | custom-call | flops 1000 | bytes 12000000 | tf_op jit(solution)/shard_map/forward/pallas_call | solution.py:436
  33.8 2.2 %rows_first.1.earlier_ref = f32[8,640]{1,0:T(8,128)S(1)} custom-call(s32[2]{0:T(128)S(1)} %bitcast.12, bf16[128,2048]{1,0:T(8,128)(2,1)S(1)} %bitcast.8, f32[128,2048]{1,0:T(8,128)S(1)} %get-tuple-element.21.refs_1_, bf16[128,2048]{1,0:T(8,128)(2,1)S(1)} %get-tuple-element.22.refs_2_, bf16[2,3,128,128]{3,2,1,0:T(8,128)(2,1)S(1)} %get-tuple-element.23.refs_3_, ...), custom_call_target="tpu_custom_call" | custom-call | flops 1000 | bytes 6000000 | tf_op jit(solution)/shard_map/rows_first/pallas_call | solution.py:487
  36.0 2.3 %collective-permute-done.g_ref = bf16[128,2048]{1,0:T(8,128)(2,1)S(1)} collective-permute-done((bf16[128,2048]{1,0:T(8,128)(2,1)S(1)}, bf16[128,2048]{1,0:T(8,128)(2,1)S(1)}, u32[]{:S(2)}, u32[]{:S(2)}) %collective-permute-start) | collective-permute-done | bytes 524320 | tf_op jit(solution)/shard_map/ppermute | solution.py:20
  38.3 2.6 %backward_last.1 = (bf16[128,2048]{1,0:T(8,128)(2,1)}, f32[8,640]{1,0:T(8,128)S(1)}) custom-call(s32[2]{0:T(128)S(1)} %bitcast.13, f32[8,640]{1,0:T(8,128)S(1)} %rows_first.1.earlier_ref, bf16[128,2048]{1,0:T(8,128)(2,1)S(1)} %collective-permute-done.g_ref, f32[128,2048]{1,0:T(8,128)S(1)} %get-tuple-element.27.slope_ref, ...), custom_call_target="tpu_custom_call" | custom-call | flops 1000 | bytes 6000000 | tf_op jit(solution)/shard_map/backward_last/pallas_call | solution.py:491
  40.8 3.5 %all-to-all-start.1 = ((bf16[4,32,2048]{2,1,0:T(8,128)(2,1)}), bf16[4,32,2048]{2,1,0:T(8,128)(2,1)S(1)}, u32[]{:S(2)}, u32[]{:S(2)}) async-start(bf16[4,32,2048]{2,1,0:T(8,128)(2,1)} %bitcast.16), calls=%async_computation.1 | async-start | bytes 1048576 | tf_op jit(solution)/shard_map/all_to_all | solution.py:501
  44.3 9.7 %all-gather = f32[32,640]{1,0:T(8,128)S(1)} all-gather(f32[8,640]{1,0:T(8,128)S(1)} %get-tuple-element.37), channel_id=2, replica_groups=mesh['pipe'=32,'tensor'=4,'dp'=4] {'dp'}, dimensions={0}, use_global_device_ids=true | all-gather | bytes 102400 | tf_op jit(solution)/shard_map/all_gather | solution.py:502
  54.0 0.0 all-to-all-done.1.x_ref
  54.0 0.9 %finish.1 = (bf16[1,1,32,8192]{3,2,1,0:T(8,128)(2,1)}, f32[1,2,8]{2,1,0:T(2,128)}, f32[1,2,8]{2,1,0:T(2,128)}, f32[1,2,512]{2,1,0:T(2,128)}) custom-call(s32[1]{0:T(128)} %bitcast.me_ref, bf16[4,32,2048]{2,1,0:T(8,128)(2,1)S(1)} %all-to-all-done.1.x_ref, f32[4,8,640]{2,1,0:T(8,128)S(1)} %bitcast.9), custom_call_target="tpu_custom_call" | custom-call | flops 1000 | bytes 1000000 | tf_op jit(solution)/shard_map/finish/pallas_call | solution.py:504
Async XLA Ops:
  0.6 6.9 %copy-start.1 = (s32[2,1,1]{0,2,1:T(1,128)S(1)}, s32[2,1,1]{0,2,1:T(1,128)}, u32[]{:S(2)}) copy-start(s32[2,1,1]{0,2,1:T(1,128)} %param.20) | copy-start | bytes 28
  0.6 6.9 %copy-start.4 = (s32[2,1,1]{0,2,1:T(1,128)S(1)}, s32[2,1,1]{0,2,1:T(1,128)}, u32[]{:S(2)}) copy-start(s32[2,1,1]{0,2,1:T(1,128)} %param.21) | copy-start | bytes 28
  0.7 6.9 %copy-start.2 = (f32[1,2,32]{2,1,0:T(2,128)S(1)}, f32[1,2,32]{2,1,0:T(2,128)}, u32[]{:S(2)}) copy-start(f32[1,2,32]{2,1,0:T(2,128)} %alog_ref.3) | copy-start | bytes 772
  0.7 6.9 %copy-start.3 = (f32[1,2,32]{2,1,0:T(2,128)S(1)}, f32[1,2,32]{2,1,0:T(2,128)}, u32[]{:S(2)}) copy-start(f32[1,2,32]{2,1,0:T(2,128)} %dskip_ref.3) | copy-start | bytes 772
  0.7 6.9 %copy-start = (f32[1,2,2048]{2,1,0:T(2,128)S(1)}, f32[1,2,2048]{2,1,0:T(2,128)}, u32[]{:S(2)}) copy-start(f32[1,2,2048]{2,1,0:T(2,128)} %gain_ref.3) | copy-start | bytes 49156
  2.5 12.0 %all-to-all-start = ((bf16[4,32,2048]{2,1,0:T(8,128)(2,1)}), bf16[4,32,2048]{2,1,0:T(8,128)(2,1)S(1)}, u32[]{:S(2)}, u32[]{:S(2)}) async-start(bf16[4,32,2048]{2,1,0:T(8,128)(2,1)} %relay_out.1), calls=%async_computation | async-start | bytes 1048576 | tf_op jit(solution)/shard_map/all_to_all | solution.py:480
  15.8 22.4 %collective-permute-start = (bf16[128,2048]{1,0:T(8,128)(2,1)S(1)}, bf16[128,2048]{1,0:T(8,128)(2,1)S(1)}, u32[]{:S(2)}, u32[]{:S(2)}) collective-permute-start(bf16[128,2048]{1,0:T(8,128)(2,1)S(1)} %backward_first.1), channel_id=1, source_target_pairs={{16,0},{32,16},{48,32},{64,48},{80,64},{96,80},{112,96},{128,112},... | collective-permute-start | bytes 1572872 | tf_op jit(solution)/shard_map/ppermute | solution.py:20
  40.8 13.2 %all-to-all-start.1 = ((bf16[4,32,2048]{2,1,0:T(8,128)(2,1)}), bf16[4,32,2048]{2,1,0:T(8,128)(2,1)S(1)}, u32[]{:S(2)}, u32[]{:S(2)}) async-start(bf16[4,32,2048]{2,1,0:T(8,128)(2,1)} %bitcast.16), calls=%async_computation.1 | async-start | bytes 1048576 | tf_op jit(solution)/shard_map/all_to_all | solution.py:501

commit v2 on v1

--- a/solution.py
+++ b/solution.py
@@ -12,6 +12,7 @@
 bf16 = jnp.bfloat16
 LANES = 128
 WIDTH = 64
+ORDERS = ((0, 1, 2, 3), (2, 0, 3, 1))
 
 
 def passed_along(block, axis, distance):
@@ -25,6 +26,11 @@
     rest = value - high.astype(f32)
     middle = rest.astype(bf16)
     return high, middle, (rest - middle.astype(f32)).astype(bf16)
+
+
+def place_of(member, core):
+    places = [order.index(member) for order in ORDERS]
+    return jnp.where(core == 0, places[0], places[1])
 
 
 def of_block(ref, block, here=slice(None)):
@@ -178,7 +184,7 @@
             slope_ref[:, here] = gate_ref[group, :, there] * scale
 
 
-def backward(g_ref, slope_ref, normed_ref, scores_ref, rows_ref, x_ref, heads_ref, scratch, dx_ref, want_rows):
+def backward(me_ref, g_ref, slope_ref, normed_ref, scores_ref, rows_ref, x_ref, heads_ref, scratch, dx_ref, want_rows):
     drive_ref, v_ref, q_ref, y_ref, part_ref, wide_ref = scratch
     seq, chan = normed_ref.shape
     groups = scores_ref.shape[0]
@@ -190,11 +196,16 @@
     one_hot = spread_map(held, width)
     found = [[], [], []]
     means = []
+    places = [place_of(member, me_ref[0] % 2) for member in range(g_ref.shape[0])]
+
+    def gradient(here):
+        return jnp.concatenate([g_ref[place, :, here] for place in places], axis=0).astype(f32)
+
     for group in range(groups):
         total = jnp.zeros((seq, LANES), f32)
         for tile in range(tiles):
             here = pl.ds(group * per_group + tile * LANES, LANES)
-            gn = g_ref[:, here].astype(f32) * normed_ref[:, here].astype(f32)
+            gn = gradient(here) * normed_ref[:, here].astype(f32)
             total = total + gn * rows_ref[0:1, here]
             if want_rows:
                 found[0].append(jnp.sum(gn, axis=0, keepdims=True))
@@ -206,7 +217,7 @@
         for tile in range(tiles):
             here = pl.ds(group * per_group + tile * LANES, LANES)
             there = pl.ds(tile * LANES, LANES)
-            g = g_ref[:, here].astype(f32)
+            g = gradient(here)
             v = slope_ref[:, here] * (g * rows_ref[0:1, here] - normed_ref[:, here].astype(f32) * means[group])
             high = v.astype(bf16)
             v_ref[group, 0:seq, there] = high
@@ -272,12 +283,12 @@
 
 
 def backward_first(*refs):
-    backward(*refs[:7], refs[8:], refs[7], False)
+    backward(*refs[:8], refs[9:], refs[8], False)
 
 
 def rows_first(block_ref, *refs):
-    heads = refs[6].shape[1] // 3
-    place_rows(backward(*refs[:7], refs[8:], None, True), block_ref[0], heads, refs[7], None)
+    heads = refs[7].shape[1] // 3
+    place_rows(backward(*refs[:8], refs[9:], None, True), block_ref[0], heads, refs[8], None)
 
 
 def backward_last(
@@ -372,12 +383,13 @@
         move.wait()
 
 
-def relay_out(x_ref, out_ref, held_ref, came, gone):
+def relay_out(me_ref, x_ref, out_ref, held_ref, came, gone):
     parts, _, share = out_ref.shape
     ins = [
         pltpu.make_async_copy(x_ref.at[0, 0, :, pl.ds(i * share, share)], held_ref.at[i], came.at[i]) for i in range(parts)
     ]
-    outs = [pltpu.make_async_copy(held_ref.at[i], out_ref.at[i], gone.at[i]) for i in range(parts)]
+    places = [place_of(i, me_ref[0] % 2) for i in range(parts)]
+    outs = [pltpu.make_async_copy(held_ref.at[i], out_ref.at[places[i]], gone.at[i]) for i in range(parts)]
     for copy in ins:
         copy.start()
     for first, second in zip(ins, outs):
@@ -472,20 +484,21 @@
     staged = call(
         relay_out,
         "relay_out",
-        [in_any],
+        [in_smem, in_any],
         in_any,
         sized((parts, tokens, share), bf16),
         [pltpu.VMEM((parts, tokens, share), bf16)] + [pltpu.SemaphoreType.DMA((parts,))] * 2,
-    )(pltpu.with_memory_space_constraint(grad_in, pltpu.HBM))
-    g = lax.all_to_all(staged, "tensor", split_axis=0, concat_axis=0, tiled=True).reshape(seq, share)
+    )(me, pltpu.with_memory_space_constraint(grad_in, pltpu.HBM))
+    groups = [[member * replicas + d for member in ORDERS[d % 2]] for d in range(replicas)]
+    g = lax.all_to_all(staged, ("tensor", "dp"), split_axis=0, concat_axis=0, axis_index_groups=groups, tiled=True)
     first, last = [
         run_forward(tick, block_table, entry_table, saved_x, saved_z, steps, saved_b, saved_c, a_log, dskip, gain)
         for tick in range(2)
     ]
     scratch = backward_scratch(seq, share, saved_b.shape[4])
-    dx = call(backward_first, "backward_first", [in_vmem] * 7, in_vmem, sized((seq, share), bf16), scratch, 20, 6)(g, *first)
-    earlier = call(rows_first, "rows_first", [in_smem] + [in_vmem] * 7, in_vmem, packet, scratch, 20, 6)(
-        block_table, g, *first
+    dx = call(backward_first, "backward_first", [in_smem] + [in_vmem] * 7, in_vmem, sized((seq, share), bf16), scratch, 20, 6)(me, g, *first)
+    earlier = call(rows_first, "rows_first", [in_smem] * 2 + [in_vmem] * 7, in_vmem, packet, scratch, 20, 6)(
+        block_table, me, g, *first
     )
     g = passed_along(dx, "pipe", -1)
     dx, rows = call(

time: 55.4 us -> 54.9 us (level)
  starting transfers between devices: 21.9 us -> 24.9 us
  waiting for transfers between devices: 5.26 us -> 2.77 us
  blocking collectives: 9.7 us -> 8.83 us
    all_to_all x1, waiting for transfers between devices: 2.98 us -> 0.04 us  [shards(): lax.all_to_all(staged, ('tensor', 'dp'), split_axis=0, concat_axis=0, axi...]
    all_to_all x1, starting transfers between devices: 5.02 us -> 7.19 us  [shards(): lax.all_to_all(staged, ('tensor', 'dp'), split_axis=0, concat_axis=0, axi...]
    all_gather x1, blocking collectives: 9.7 us -> 8.83 us  [shards(): rows = lax.all_gather(rows, 'dp')]
  transfers between devices with their start and end apart: 3 -> 3, of which waited for: 2 -> 1; matrix products, arithmetic and copies ran while one was open for 0% -> 0% of each run, Pallas kernels for 19% -> 20%
where the time goes in v2:
time: 54.9 us; the launch traced here: 54.6 us
  starting transfers between devices  24.9 us (45%)
  Pallas kernels  17.2 us (31%)
  blocking collectives  8.83 us (16%)
  waiting for transfers between devices  2.77 us (5%)
  between operations  0.75 us (1%)
    ppermute x1, starting transfers between devices, passed_along(): return lax.ppermute(block, axis, route)  13.9 us
    all_gather x1, blocking collectives, shards(): rows = lax.all_gather(rows, 'dp')  8.83 us
    pallas_call x2, Pallas kernels, run_forward(): call(partial(forward, tick), 'forward', in_specs, [in_vmem] * len(outs),...  8.46 us
    all_to_all x1, starting transfers between devices, shards(): lax.all_to_all(staged, ('tensor', 'dp'), split_axis=0, concat_axis=0, axi...  7.19 us
    all_to_all x1, starting transfers between devices, shards(): lax.all_to_all(dx.reshape(parts, tokens, share), 'tensor', split_axis=0,...  3.87 us
    ppermute x1, waiting for transfers between devices, passed_along(): return lax.ppermute(block, axis, route)  2.72 us
    pallas_call x1, Pallas kernels, shards(): call(backward_last, 'backward_last', [in_smem] + [in_vmem] * 11, [in_any,...  2.4 us
    pallas_call x1, Pallas kernels, shards(): call(rows_first, 'rows_first', [in_smem] * 2 + [in_vmem] * 7, in_vmem, pa...  2.23 us
  transfers between devices with their start and end apart: 3, of which 1 were waited for; matrix products, arithmetic and copies ran while one was open for 0% of the time, Pallas kernels for 20%

profile of v2, /device:TPU:1, one launch (start us, length us, event | category | flops | bytes accessed | tf_op | source)
XLA Modules:
  0.0 54.6 jit_solution(3247377661034418246)
XLA Ops:
  0.6 0.0 copy-start
  0.6 0.0 copy-start.3
  0.7 0.0 copy-start.2
  0.7 0.0 copy-start.4
  0.7 0.0 copy-start.1
  0.7 1.8 %relay_out.1 = bf16[4,32,2048]{2,1,0:T(8,128)(2,1)} custom-call(s32[1]{0:T(128)} %bitcast.me_ref.refs_0_, bf16[1,1,32,8192]{3,2,1,0:T(8,128)(2,1)} %x_ref.1), custom_call_target="tpu_custom_call" | custom-call | flops 1000 | bytes 1000000 | tf_op jit(solution)/shard_map/relay_out/pallas_call | solution.py:484
  2.5 7.2 %all-to-all-start = ((bf16[4,32,2048]{2,1,0:T(8,128)(2,1)}), bf16[4,32,2048]{2,1,0:T(8,128)(2,1)S(1)}, u32[]{:S(2)}, u32[]{:S(2)}) async-start(bf16[4,32,2048]{2,1,0:T(8,128)(2,1)} %relay_out.1), calls=%async_computation | async-start | bytes 1048576 | tf_op jit(solution)/shard_map/all_to_all | solution.py:493
  9.7 0.0 copy-done
  9.7 0.0 copy-done.3
  9.7 0.0 copy-done.2
  9.7 0.0 copy-done.4
  9.8 0.0 copy-done.1
  9.8 3.9 %forward.2 = (f32[128,2048]{1,0:T(8,128)S(1)}, bf16[128,2048]{1,0:T(8,128)(2,1)S(1)}, bf16[2,3,128,128]{3,2,1,0:T(8,128)(2,1)S(1)}, f32[2,2048]{1,0:T(2,128)S(1)...) custom-call(s32[2]{0:T(128)S(1)} %bitcast.7, s32[2]{0:T(128)S(1)} %bitcast.11, ...), custom_call_target="tpu_custom_call" | custom-call | flops 1000 | bytes 12000000 | tf_op jit(solution)/shard_map/forward/pallas_call | solution.py:448
  13.7 0.0 all-to-all-done.refs_1_
  13.7 1.4 %backward_first.1 = bf16[128,2048]{1,0:T(8,128)(2,1)S(1)} custom-call(s32[1]{0:T(128)} %bitcast.me_ref.refs_0_, bf16[4,32,2048]{2,1,0:T(8,128)(2,1)S(1)} %all-to-all-done.refs_1_, f32[128,2048]{1,0:T(8,128)S(1)} %get-tuple-element.21.refs_2_, bf16[128,2048]{1,0:T(8,128)(2,1)S(1)} %get-tuple-element.22.refs_3_, ...), custom_call_target="tpu_custom_call" | custom-call | flops 1000 | bytes 6000000 | tf_op jit(solution)/shard_map/backward_first/pallas_call | solution.py:499
  15.1 13.9 %collective-permute-start = (bf16[128,2048]{1,0:T(8,128)(2,1)S(1)}, bf16[128,2048]{1,0:T(8,128)(2,1)S(1)}, u32[]{:S(2)}, u32[]{:S(2)}) collective-permute-start(bf16[128,2048]{1,0:T(8,128)(2,1)S(1)} %backward_first.1), channel_id=1, source_target_pairs={{16,0},{32,16},{48,32},{64,48},{80,64},{96,80},{112,96},{128,112},... | collective-permute-start | bytes 1572872 | tf_op jit(solution)/shard_map/ppermute | solution.py:21
  29.0 4.6 %forward.3 = (f32[128,2048]{1,0:T(8,128)S(1)}, bf16[128,2048]{1,0:T(8,128)(2,1)S(1)}, bf16[2,3,128,128]{3,2,1,0:T(8,128)(2,1)S(1)}, f32[2,2048]{1,0:T(2,128)S(1)...) custom-call(s32[2]{0:T(128)S(1)} %bitcast.8, ...), custom_call_target="tpu_custom_call" | custom-call | flops 1000 | bytes 12000000 | tf_op jit(solution)/shard_map/forward/pallas_call | solution.py:448
  33.5 2.2 %rows_first.1.earlier_ref = f32[8,640]{1,0:T(8,128)S(1)} custom-call(s32[2]{0:T(128)S(1)} %bitcast.9, s32[1]{0:T(128)} %bitcast.me_ref.refs_0_, bf16[4,32,2048]{2,1,0:T(8,128)(2,1)S(1)} %all-to-all-done.refs_1_, f32[128,2048]{1,0:T(8,128)S(1)} %get-tuple-element.21.refs_2_, bf16[128,2048]{1,0:T(8,128)(2,1)S(1)} %get-tuple-element.22.refs_3_, ...), custom_call_target="tpu_custom_call" | custom-call | flops 1000 | bytes 6000000 | tf_op jit(solution)/shard_map/rows_first/pallas_call | solution.py:500
  35.8 2.7 %collective-permute-done.g_ref = bf16[128,2048]{1,0:T(8,128)(2,1)S(1)} collective-permute-done((bf16[128,2048]{1,0:T(8,128)(2,1)S(1)}, bf16[128,2048]{1,0:T(8,128)(2,1)S(1)}, u32[]{:S(2)}, u32[]{:S(2)}) %collective-permute-start) | collective-permute-done | bytes 524320 | tf_op jit(solution)/shard_map/ppermute | solution.py:21
  38.5 2.4 %backward_last.1 = (bf16[128,2048]{1,0:T(8,128)(2,1)}, f32[8,640]{1,0:T(8,128)S(1)}) custom-call(s32[2]{0:T(128)S(1)} %bitcast.10, f32[8,640]{1,0:T(8,128)S(1)} %rows_first.1.earlier_ref, bf16[128,2048]{1,0:T(8,128)(2,1)S(1)} %collective-permute-done.g_ref, f32[128,2048]{1,0:T(8,128)S(1)} %get-tuple-element.27.slope_ref, ...), custom_call_target="tpu_custom_call" | custom-call | flops 1000 | bytes 6000000 | tf_op jit(solution)/shard_map/backward_last/pallas_call | solution.py:504
  40.9 3.9 %all-to-all-start.1 = ((bf16[4,32,2048]{2,1,0:T(8,128)(2,1)}), bf16[4,32,2048]{2,1,0:T(8,128)(2,1)S(1)}, u32[]{:S(2)}, u32[]{:S(2)}) async-start(bf16[4,32,2048]{2,1,0:T(8,128)(2,1)} %bitcast.13), calls=%async_computation.1 | async-start | bytes 1048576 | tf_op jit(solution)/shard_map/all_to_all | solution.py:514
  44.8 8.8 %all-gather = f32[32,640]{1,0:T(8,128)S(1)} all-gather(f32[8,640]{1,0:T(8,128)S(1)} %get-tuple-element.37), channel_id=2, replica_groups=mesh['pipe'=32,'tensor'=4,'dp'=4] {'dp'}, dimensions={0}, use_global_device_ids=true | all-gather | bytes 102400 | tf_op jit(solution)/shard_map/all_gather | solution.py:515
  53.6 0.0 all-to-all-done.1.x_ref
  53.6 0.9 %finish.1 = (bf16[1,1,32,8192]{3,2,1,0:T(8,128)(2,1)}, f32[1,2,8]{2,1,0:T(2,128)}, f32[1,2,8]{2,1,0:T(2,128)}, f32[1,2,512]{2,1,0:T(2,128)}) custom-call(s32[1]{0:T(128)} %bitcast.me_ref.refs_0_, bf16[4,32,2048]{2,1,0:T(8,128)(2,1)S(1)} %all-to-all-done.1.x_ref, f32[4,8,640]{2,1,0:T(8,128)S(1)} %bitcast.6), custom_call_target="tpu_custom_call" | custom-call | flops 1000 | bytes 1000000 | tf_op jit(solution)/shard_map/finish/pallas_call | solution.py:517
Async XLA Ops:
  0.6 9.1 %copy-start = (f32[1,2,2048]{2,1,0:T(2,128)S(1)}, f32[1,2,2048]{2,1,0:T(2,128)}, u32[]{:S(2)}) copy-start(f32[1,2,2048]{2,1,0:T(2,128)} %gain_ref.3) | copy-start | bytes 49156
  0.6 9.1 %copy-start.3 = (f32[1,2,32]{2,1,0:T(2,128)S(1)}, f32[1,2,32]{2,1,0:T(2,128)}, u32[]{:S(2)}) copy-start(f32[1,2,32]{2,1,0:T(2,128)} %dskip_ref.3) | copy-start | bytes 772
  0.7 9.1 %copy-start.2 = (f32[1,2,32]{2,1,0:T(2,128)S(1)}, f32[1,2,32]{2,1,0:T(2,128)}, u32[]{:S(2)}) copy-start(f32[1,2,32]{2,1,0:T(2,128)} %alog_ref.3) | copy-start | bytes 772
  0.7 9.1 %copy-start.4 = (s32[2,1,1]{0,2,1:T(1,128)S(1)}, s32[2,1,1]{0,2,1:T(1,128)}, u32[]{:S(2)}) copy-start(s32[2,1,1]{0,2,1:T(1,128)} %param.21) | copy-start | bytes 28
  0.7 9.1 %copy-start.1 = (s32[2,1,1]{0,2,1:T(1,128)S(1)}, s32[2,1,1]{0,2,1:T(1,128)}, u32[]{:S(2)}) copy-start(s32[2,1,1]{0,2,1:T(1,128)} %param.20) | copy-start | bytes 28
  2.5 11.2 %all-to-all-start = ((bf16[4,32,2048]{2,1,0:T(8,128)(2,1)}), bf16[4,32,2048]{2,1,0:T(8,128)(2,1)S(1)}, u32[]{:S(2)}, u32[]{:S(2)}) async-start(bf16[4,32,2048]{2,1,0:T(8,128)(2,1)} %relay_out.1), calls=%async_computation | async-start | bytes 1048576 | tf_op jit(solution)/shard_map/all_to_all | solution.py:493
  15.1 23.4 %collective-permute-start = (bf16[128,2048]{1,0:T(8,128)(2,1)S(1)}, bf16[128,2048]{1,0:T(8,128)(2,1)S(1)}, u32[]{:S(2)}, u32[]{:S(2)}) collective-permute-start(bf16[128,2048]{1,0:T(8,128)(2,1)S(1)} %backward_first.1), channel_id=1, source_target_pairs={{16,0},{32,16},{48,32},{64,48},{80,64},{96,80},{112,96},{128,112},... | collective-permute-start | bytes 1572872 | tf_op jit(solution)/shard_map/ppermute | solution.py:21
  40.9 12.7 %all-to-all-start.1 = ((bf16[4,32,2048]{2,1,0:T(8,128)(2,1)}), bf16[4,32,2048]{2,1,0:T(8,128)(2,1)S(1)}, u32[]{:S(2)}, u32[]{:S(2)}) async-start(bf16[4,32,2048]{2,1,0:T(8,128)(2,1)} %bitcast.13), calls=%async_computation.1 | async-start | bytes 1048576 | tf_op jit(solution)/shard_map/all_to_all | solution.py:514

commit v3 on v2

--- a/solution.py
+++ b/solution.py
@@ -76,7 +76,7 @@
     *refs,
 ):
     if tick:
-        wx_out, skips_ref, moved_ref, mixed_ref, driven_ref, wide_ref, x_ref, *refs = refs
+        wx_out, skips_ref, moved_ref, mixed_ref, driven_ref, pushed_ref, wide_ref, x_ref, *refs = refs
     else:
         x_ref, heads_ref, *refs = refs
     z_ref, dt_ref, b_ref, c_ref, drive_ref, wx_ref, ec_ref, y_ref, gated_ref, gate_ref, sem = refs
@@ -180,8 +180,14 @@
         for tile in range(tiles):
             here = pl.ds(group * per_group + tile * LANES, LANES)
             there = pl.ds(tile * LANES, LANES)
-            normed_ref[:, here] = (gated_ref[group, :, there] * scale).astype(bf16)
-            slope_ref[:, here] = gate_ref[group, :, there] * scale
+            normed = (gated_ref[group, :, there] * scale).astype(bf16)
+            slope = gate_ref[group, :, there] * scale
+            normed_ref[:, here] = normed
+            if tick:
+                slope_ref[:, here] = slope * rows_ref[0:1, here]
+                pushed_ref[:, here] = slope * normed.astype(f32)
+            else:
+                slope_ref[:, here] = slope
 
 
 def backward(me_ref, g_ref, slope_ref, normed_ref, scores_ref, rows_ref, x_ref, heads_ref, scratch, dx_ref, want_rows):
@@ -304,6 +310,7 @@
     moved_ref,
     mixed_ref,
     driven_ref,
+    pushed_ref,
     out_ref,
     packet_ref,
     dx_ref,
@@ -330,7 +337,7 @@
             here = pl.ds(group * per_group + tile * LANES, LANES)
             there = pl.ds(tile * LANES, LANES)
             g = g_ref[:, here].astype(f32)
-            v = slope_ref[:, here] * (g * gain_ref[0:1, here] - normed_ref[:, here].astype(f32) * mean)
+            v = slope_ref[:, here] * g - pushed_ref[:, here] * mean
             v_ref[group, :, there] = v.astype(bf16)
             part_ref[group, :, there] = g + skips_ref[:, here] * v
             found[1].append(jnp.sum(moved_ref[:, here] * v, axis=0, keepdims=True))
@@ -430,7 +437,7 @@
     flat = sized((seq, chan), f32)
     outs = [flat, sized((seq, chan), bf16), sized((groups, 3, seq, seq), bf16), sized((2, chan), f32)]
     if tick:
-        outs += [flat] * 5
+        outs += [flat] * 6
         scratch = [pltpu.VMEM((groups, 2 * seq, chan // groups), f32), pltpu.VMEM((seq, chan), bf16)]
     else:
         outs += [sized((seq, chan), bf16), sized((seq, 3 * heads), f32)]
@@ -504,7 +511,7 @@
     dx, rows = call(
         backward_last,
         "backward_last",
-        [in_smem] + [in_vmem] * 11,
+        [in_smem] + [in_vmem] * 12,
         [in_any, in_vmem],
         [pltpu.HBM((seq, share), bf16), packet],
         [pltpu.VMEM((seq, share), bf16), scratch[0], *scratch[2:4], pltpu.SemaphoreType.DMA((saved_b.shape[4],))],

time: 54.9 us -> 54.9 us (level)
  transfers between devices with their start and end apart: 3 -> 3, of which waited for: 1 -> 2; matrix products, arithmetic and copies ran while one was open for 0% -> 0% of each run, Pallas kernels for 20% -> 20%
where the time goes in v3:
time: 54.9 us; the launch traced here: 54.5 us
  starting transfers between devices  24.9 us (45%)
  Pallas kernels  17.3 us (32%)
  blocking collectives  8.84 us (16%)
  waiting for transfers between devices  2.6 us (5%)
  between operations  0.75 us (1%)
    ppermute x1, starting transfers between devices, passed_along(): return lax.ppermute(block, axis, route)  13.9 us
    all_gather x1, blocking collectives, shards(): rows = lax.all_gather(rows, 'dp')  8.84 us
    pallas_call x2, Pallas kernels, run_forward(): call(partial(forward, tick), 'forward', in_specs, [in_vmem] * len(outs),...  8.65 us
    all_to_all x1, starting transfers between devices, shards(): lax.all_to_all(staged, ('tensor', 'dp'), split_axis=0, concat_axis=0, axi...  7.19 us
    all_to_all x1, starting transfers between devices, shards(): lax.all_to_all(dx.reshape(parts, tokens, share), 'tensor', split_axis=0,...  3.87 us
    ppermute x1, waiting for transfers between devices, passed_along(): return lax.ppermute(block, axis, route)  2.54 us
    pallas_call x1, Pallas kernels, shards(): call(backward_last, 'backward_last', [in_smem] + [in_vmem] * 12, [in_any,...  2.33 us
    pallas_call x1, Pallas kernels, shards(): call(rows_first, 'rows_first', [in_smem] * 2 + [in_vmem] * 7, in_vmem, pa...  2.21 us
  transfers between devices with their start and end apart: 3, of which 2 were waited for; matrix products, arithmetic and copies ran while one was open for 0% of the time, Pallas kernels for 20%

profile of v3, /device:TPU:1, one launch (start us, length us, event | category | flops | bytes accessed | tf_op | source)
XLA Modules:
  0.0 54.5 jit_solution(14355931567859886098)
XLA Ops:
  0.6 0.0 copy-start
  0.6 0.0 copy-start.3
  0.7 0.0 copy-start.2
  0.7 0.0 copy-start.4
  0.7 0.0 copy-start.1
  0.7 1.8 %relay_out.1 = bf16[4,32,2048]{2,1,0:T(8,128)(2,1)} custom-call(s32[1]{0:T(128)} %bitcast.me_ref.refs_0_, bf16[1,1,32,8192]{3,2,1,0:T(8,128)(2,1)} %x_ref.1), custom_call_target="tpu_custom_call" | custom-call | flops 1000 | bytes 1000000 | tf_op jit(solution)/shard_map/relay_out/pallas_call | solution.py:491
  2.5 7.2 %all-to-all-start = ((bf16[4,32,2048]{2,1,0:T(8,128)(2,1)}), bf16[4,32,2048]{2,1,0:T(8,128)(2,1)S(1)}, u32[]{:S(2)}, u32[]{:S(2)}) async-start(bf16[4,32,2048]{2,1,0:T(8,128)(2,1)} %relay_out.1), calls=%async_computation | async-start | bytes 1048576 | tf_op jit(solution)/shard_map/all_to_all | solution.py:500
  9.7 0.0 copy-done
  9.7 0.0 copy-done.3
  9.7 0.0 copy-done.2
  9.7 0.0 copy-done.4
  9.8 0.0 copy-done.1
  9.8 3.9 %forward.2 = (f32[128,2048]{1,0:T(8,128)S(1)}, bf16[128,2048]{1,0:T(8,128)(2,1)S(1)}, bf16[2,3,128,128]{3,2,1,0:T(8,128)(2,1)S(1)}, f32[2,2048]{1,0:T(2,128)S(1)...) custom-call(s32[2]{0:T(128)S(1)} %bitcast.7, s32[2]{0:T(128)S(1)} %bitcast.11, ...), custom_call_target="tpu_custom_call" | custom-call | flops 1000 | bytes 12000000 | tf_op jit(solution)/shard_map/forward/pallas_call | solution.py:455
  13.7 0.1 all-to-all-done.refs_1_
  13.7 1.4 %backward_first.1 = bf16[128,2048]{1,0:T(8,128)(2,1)S(1)} custom-call(s32[1]{0:T(128)} %bitcast.me_ref.refs_0_, bf16[4,32,2048]{2,1,0:T(8,128)(2,1)S(1)} %all-to-all-done.refs_1_, f32[128,2048]{1,0:T(8,128)S(1)} %get-tuple-element.22.refs_2_, bf16[128,2048]{1,0:T(8,128)(2,1)S(1)} %get-tuple-element.23.refs_3_, ...), custom_call_target="tpu_custom_call" | custom-call | flops 1000 | bytes 6000000 | tf_op jit(solution)/shard_map/backward_first/pallas_call | solution.py:506
  15.1 13.9 %collective-permute-start = (bf16[128,2048]{1,0:T(8,128)(2,1)S(1)}, bf16[128,2048]{1,0:T(8,128)(2,1)S(1)}, u32[]{:S(2)}, u32[]{:S(2)}) collective-permute-start(bf16[128,2048]{1,0:T(8,128)(2,1)S(1)} %backward_first.1), channel_id=1, source_target_pairs={{16,0},{32,16},{48,32},{64,48},{80,64},{96,80},{112,96},{128,112},... | collective-permute-start | bytes 1572872 | tf_op jit(solution)/shard_map/ppermute | solution.py:21
  29.0 4.8 %forward.3 = (f32[128,2048]{1,0:T(8,128)S(1)}, bf16[128,2048]{1,0:T(8,128)(2,1)S(1)}, bf16[2,3,128,128]{3,2,1,0:T(8,128)(2,1)S(1)}, f32[2,2048]{1,0:T(2,128)S(1)...) custom-call(s32[2]{0:T(128)S(1)} %bitcast.8, ...), custom_call_target="tpu_custom_call" | custom-call | flops 1000 | bytes 12000000 | tf_op jit(solution)/shard_map/forward/pallas_call | solution.py:455
  33.7 2.2 %rows_first.1.earlier_ref = f32[8,640]{1,0:T(8,128)S(1)} custom-call(s32[2]{0:T(128)S(1)} %bitcast.9, s32[1]{0:T(128)} %bitcast.me_ref.refs_0_, bf16[4,32,2048]{2,1,0:T(8,128)(2,1)S(1)} %all-to-all-done.refs_1_, f32[128,2048]{1,0:T(8,128)S(1)} %get-tuple-element.22.refs_2_, bf16[128,2048]{1,0:T(8,128)(2,1)S(1)} %get-tuple-element.23.refs_3_, ...), custom_call_target="tpu_custom_call" | custom-call | flops 1000 | bytes 6000000 | tf_op jit(solution)/shard_map/rows_first/pallas_call | solution.py:507
  36.0 2.5 %collective-permute-done.g_ref = bf16[128,2048]{1,0:T(8,128)(2,1)S(1)} collective-permute-done((bf16[128,2048]{1,0:T(8,128)(2,1)S(1)}, bf16[128,2048]{1,0:T(8,128)(2,1)S(1)}, u32[]{:S(2)}, u32[]{:S(2)}) %collective-permute-start) | collective-permute-done | bytes 524320 | tf_op jit(solution)/shard_map/ppermute | solution.py:21
  38.5 2.3 %backward_last.1 = (bf16[128,2048]{1,0:T(8,128)(2,1)}, f32[8,640]{1,0:T(8,128)S(1)}) custom-call(s32[2]{0:T(128)S(1)} %bitcast.10, f32[8,640]{1,0:T(8,128)S(1)} %rows_first.1.earlier_ref, bf16[128,2048]{1,0:T(8,128)(2,1)S(1)} %collective-permute-done.g_ref, f32[128,2048]{1,0:T(8,128)S(1)} %get-tuple-element.28.slope_ref, ...), custom_call_target="tpu_custom_call" | custom-call | flops 1000 | bytes 6000000 | tf_op jit(solution)/shard_map/backward_last/pallas_call | solution.py:511
  40.8 3.9 %all-to-all-start.1 = ((bf16[4,32,2048]{2,1,0:T(8,128)(2,1)}), bf16[4,32,2048]{2,1,0:T(8,128)(2,1)S(1)}, u32[]{:S(2)}, u32[]{:S(2)}) async-start(bf16[4,32,2048]{2,1,0:T(8,128)(2,1)} %bitcast.13), calls=%async_computation.1 | async-start | bytes 1048576 | tf_op jit(solution)/shard_map/all_to_all | solution.py:521
  44.7 8.8 %all-gather = f32[32,640]{1,0:T(8,128)S(1)} all-gather(f32[8,640]{1,0:T(8,128)S(1)} %get-tuple-element.39), channel_id=2, replica_groups=mesh['pipe'=32,'tensor'=4,'dp'=4] {'dp'}, dimensions={0}, use_global_device_ids=true | all-gather | bytes 102400 | tf_op jit(solution)/shard_map/all_gather | solution.py:522
  53.6 0.0 all-to-all-done.1.x_ref
  53.6 0.9 %finish.1 = (bf16[1,1,32,8192]{3,2,1,0:T(8,128)(2,1)}, f32[1,2,8]{2,1,0:T(2,128)}, f32[1,2,8]{2,1,0:T(2,128)}, f32[1,2,512]{2,1,0:T(2,128)}) custom-call(s32[1]{0:T(128)} %bitcast.me_ref.refs_0_, bf16[4,32,2048]{2,1,0:T(8,128)(2,1)S(1)} %all-to-all-done.1.x_ref, f32[4,8,640]{2,1,0:T(8,128)S(1)} %bitcast.6), custom_call_target="tpu_custom_call" | custom-call | flops 1000 | bytes 1000000 | tf_op jit(solution)/shard_map/finish/pallas_call | solution.py:524
Async XLA Ops:
  0.6 9.1 %copy-start = (f32[1,2,2048]{2,1,0:T(2,128)S(1)}, f32[1,2,2048]{2,1,0:T(2,128)}, u32[]{:S(2)}) copy-start(f32[1,2,2048]{2,1,0:T(2,128)} %gain_ref.3) | copy-start | bytes 49156
  0.6 9.1 %copy-start.3 = (f32[1,2,32]{2,1,0:T(2,128)S(1)}, f32[1,2,32]{2,1,0:T(2,128)}, u32[]{:S(2)}) copy-start(f32[1,2,32]{2,1,0:T(2,128)} %dskip_ref.3) | copy-start | bytes 772
  0.7 9.1 %copy-start.2 = (f32[1,2,32]{2,1,0:T(2,128)S(1)}, f32[1,2,32]{2,1,0:T(2,128)}, u32[]{:S(2)}) copy-start(f32[1,2,32]{2,1,0:T(2,128)} %alog_ref.3) | copy-start | bytes 772
  0.7 9.1 %copy-start.4 = (s32[2,1,1]{0,2,1:T(1,128)S(1)}, s32[2,1,1]{0,2,1:T(1,128)}, u32[]{:S(2)}) copy-start(s32[2,1,1]{0,2,1:T(1,128)} %param.21) | copy-start | bytes 28
  0.7 9.1 %copy-start.1 = (s32[2,1,1]{0,2,1:T(1,128)S(1)}, s32[2,1,1]{0,2,1:T(1,128)}, u32[]{:S(2)}) copy-start(s32[2,1,1]{0,2,1:T(1,128)} %param.20) | copy-start | bytes 28
  2.5 11.2 %all-to-all-start = ((bf16[4,32,2048]{2,1,0:T(8,128)(2,1)}), bf16[4,32,2048]{2,1,0:T(8,128)(2,1)S(1)}, u32[]{:S(2)}, u32[]{:S(2)}) async-start(bf16[4,32,2048]{2,1,0:T(8,128)(2,1)} %relay_out.1), calls=%async_computation | async-start | bytes 1048576 | tf_op jit(solution)/shard_map/all_to_all | solution.py:500
  15.1 23.4 %collective-permute-start = (bf16[128,2048]{1,0:T(8,128)(2,1)S(1)}, bf16[128,2048]{1,0:T(8,128)(2,1)S(1)}, u32[]{:S(2)}, u32[]{:S(2)}) collective-permute-start(bf16[128,2048]{1,0:T(8,128)(2,1)S(1)} %backward_first.1), channel_id=1, source_target_pairs={{16,0},{32,16},{48,32},{64,48},{80,64},{96,80},{112,96},{128,112},... | collective-permute-start | bytes 1572872 | tf_op jit(solution)/shard_map/ppermute | solution.py:21
  40.8 12.7 %all-to-all-start.1 = ((bf16[4,32,2048]{2,1,0:T(8,128)(2,1)}), bf16[4,32,2048]{2,1,0:T(8,128)(2,1)S(1)}, u32[]{:S(2)}, u32[]{:S(2)}) async-start(bf16[4,32,2048]{2,1,0:T(8,128)(2,1)} %bitcast.13), calls=%async_computation.1 | async-start | bytes 1048576 | tf_op jit(solution)/shard_map/all_to_all | solution.py:521

commit v4 on v3

--- a/solution.py
+++ b/solution.py
@@ -342,7 +342,6 @@
             part_ref[group, :, there] = g + skips_ref[:, here] * v
             found[1].append(jnp.sum(moved_ref[:, here] * v, axis=0, keepdims=True))
         q_ref[group] = jnp.dot(scores_ref[group, 1], v_ref[group], preferred_element_type=f32)
-    for group in range(groups):
         for tile in range(tiles):
             here = pl.ds(group * per_group + tile * LANES, LANES)
             there = pl.ds(tile * LANES, LANES)

time: 54.9 us -> 54.9 us (level)
  no operation moved by 1% of the time
where the time goes in v4:
time: 54.9 us; the launch traced here: 54.5 us
  starting transfers between devices  24.9 us (45%)
  Pallas kernels  17.3 us (32%)
  blocking collectives  8.84 us (16%)
  waiting for transfers between devices  2.6 us (5%)
  between operations  0.75 us (1%)
    ppermute x1, starting transfers between devices, passed_along(): return lax.ppermute(block, axis, route)  13.9 us
    all_gather x1, blocking collectives, shards(): rows = lax.all_gather(rows, 'dp')  8.84 us
    pallas_call x2, Pallas kernels, run_forward(): call(partial(forward, tick), 'forward', in_specs, [in_vmem] * len(outs),...  8.65 us
    all_to_all x1, starting transfers between devices, shards(): lax.all_to_all(staged, ('tensor', 'dp'), split_axis=0, concat_axis=0, axi...  7.19 us
    all_to_all x1, starting transfers between devices, shards(): lax.all_to_all(dx.reshape(parts, tokens, share), 'tensor', split_axis=0,...  3.87 us
    ppermute x1, waiting for transfers between devices, passed_along(): return lax.ppermute(block, axis, route)  2.54 us
    pallas_call x1, Pallas kernels, shards(): call(backward_last, 'backward_last', [in_smem] + [in_vmem] * 12, [in_any,...  2.33 us
    pallas_call x1, Pallas kernels, shards(): call(rows_first, 'rows_first', [in_smem] * 2 + [in_vmem] * 7, in_vmem, pa...  2.21 us
  transfers between devices with their start and end apart: 3, of which 2 were waited for; matrix products, arithmetic and copies ran while one was open for 0% of the time, Pallas kernels for 20%

profile of v4, /device:TPU:1, one launch (start us, length us, event | category | flops | bytes accessed | tf_op | source)
XLA Modules:
  0.0 54.5 jit_solution(14355931567859886098)
XLA Ops:
  0.6 0.0 copy-start
  0.6 0.0 copy-start.3
  0.7 0.0 copy-start.2
  0.7 0.0 copy-start.4
  0.7 0.0 copy-start.1
  0.7 1.8 %relay_out.1 = bf16[4,32,2048]{2,1,0:T(8,128)(2,1)} custom-call(s32[1]{0:T(128)} %bitcast.me_ref.refs_0_, bf16[1,1,32,8192]{3,2,1,0:T(8,128)(2,1)} %x_ref.1), custom_call_target="tpu_custom_call" | custom-call | flops 1000 | bytes 1000000 | tf_op jit(solution)/shard_map/relay_out/pallas_call | solution.py:490
  2.5 7.2 %all-to-all-start = ((bf16[4,32,2048]{2,1,0:T(8,128)(2,1)}), bf16[4,32,2048]{2,1,0:T(8,128)(2,1)S(1)}, u32[]{:S(2)}, u32[]{:S(2)}) async-start(bf16[4,32,2048]{2,1,0:T(8,128)(2,1)} %relay_out.1), calls=%async_computation | async-start | bytes 1048576 | tf_op jit(solution)/shard_map/all_to_all | solution.py:499
  9.7 0.0 copy-done
  9.7 0.0 copy-done.3
  9.7 0.0 copy-done.2
  9.7 0.0 copy-done.4
  9.8 0.0 copy-done.1
  9.8 3.9 %forward.2 = (f32[128,2048]{1,0:T(8,128)S(1)}, bf16[128,2048]{1,0:T(8,128)(2,1)S(1)}, bf16[2,3,128,128]{3,2,1,0:T(8,128)(2,1)S(1)}, f32[2,2048]{1,0:T(2,128)S(1)...) custom-call(s32[2]{0:T(128)S(1)} %bitcast.7, s32[2]{0:T(128)S(1)} %bitcast.11, ...), custom_call_target="tpu_custom_call" | custom-call | flops 1000 | bytes 12000000 | tf_op jit(solution)/shard_map/forward/pallas_call | solution.py:454
  13.7 0.1 all-to-all-done.refs_1_
  13.7 1.4 %backward_first.1 = bf16[128,2048]{1,0:T(8,128)(2,1)S(1)} custom-call(s32[1]{0:T(128)} %bitcast.me_ref.refs_0_, bf16[4,32,2048]{2,1,0:T(8,128)(2,1)S(1)} %all-to-all-done.refs_1_, f32[128,2048]{1,0:T(8,128)S(1)} %get-tuple-element.22.refs_2_, bf16[128,2048]{1,0:T(8,128)(2,1)S(1)} %get-tuple-element.23.refs_3_, ...), custom_call_target="tpu_custom_call" | custom-call | flops 1000 | bytes 6000000 | tf_op jit(solution)/shard_map/backward_first/pallas_call | solution.py:505
  15.1 13.9 %collective-permute-start = (bf16[128,2048]{1,0:T(8,128)(2,1)S(1)}, bf16[128,2048]{1,0:T(8,128)(2,1)S(1)}, u32[]{:S(2)}, u32[]{:S(2)}) collective-permute-start(bf16[128,2048]{1,0:T(8,128)(2,1)S(1)} %backward_first.1), channel_id=1, source_target_pairs={{16,0},{32,16},{48,32},{64,48},{80,64},{96,80},{112,96},{128,112},... | collective-permute-start | bytes 1572872 | tf_op jit(solution)/shard_map/ppermute | solution.py:21
  29.0 4.8 %forward.3 = (f32[128,2048]{1,0:T(8,128)S(1)}, bf16[128,2048]{1,0:T(8,128)(2,1)S(1)}, bf16[2,3,128,128]{3,2,1,0:T(8,128)(2,1)S(1)}, f32[2,2048]{1,0:T(2,128)S(1)...) custom-call(s32[2]{0:T(128)S(1)} %bitcast.8, ...), custom_call_target="tpu_custom_call" | custom-call | flops 1000 | bytes 12000000 | tf_op jit(solution)/shard_map/forward/pallas_call | solution.py:454
  33.7 2.2 %rows_first.1.earlier_ref = f32[8,640]{1,0:T(8,128)S(1)} custom-call(s32[2]{0:T(128)S(1)} %bitcast.9, s32[1]{0:T(128)} %bitcast.me_ref.refs_0_, bf16[4,32,2048]{2,1,0:T(8,128)(2,1)S(1)} %all-to-all-done.refs_1_, f32[128,2048]{1,0:T(8,128)S(1)} %get-tuple-element.22.refs_2_, bf16[128,2048]{1,0:T(8,128)(2,1)S(1)} %get-tuple-element.23.refs_3_, ...), custom_call_target="tpu_custom_call" | custom-call | flops 1000 | bytes 6000000 | tf_op jit(solution)/shard_map/rows_first/pallas_call | solution.py:506
  36.0 2.5 %collective-permute-done.g_ref = bf16[128,2048]{1,0:T(8,128)(2,1)S(1)} collective-permute-done((bf16[128,2048]{1,0:T(8,128)(2,1)S(1)}, bf16[128,2048]{1,0:T(8,128)(2,1)S(1)}, u32[]{:S(2)}, u32[]{:S(2)}) %collective-permute-start) | collective-permute-done | bytes 524320 | tf_op jit(solution)/shard_map/ppermute | solution.py:21
  38.5 2.3 %backward_last.1 = (bf16[128,2048]{1,0:T(8,128)(2,1)}, f32[8,640]{1,0:T(8,128)S(1)}) custom-call(s32[2]{0:T(128)S(1)} %bitcast.10, f32[8,640]{1,0:T(8,128)S(1)} %rows_first.1.earlier_ref, bf16[128,2048]{1,0:T(8,128)(2,1)S(1)} %collective-permute-done.g_ref, f32[128,2048]{1,0:T(8,128)S(1)} %get-tuple-element.28.slope_ref, ...), custom_call_target="tpu_custom_call" | custom-call | flops 1000 | bytes 6000000 | tf_op jit(solution)/shard_map/backward_last/pallas_call | solution.py:510
  40.8 3.9 %all-to-all-start.1 = ((bf16[4,32,2048]{2,1,0:T(8,128)(2,1)}), bf16[4,32,2048]{2,1,0:T(8,128)(2,1)S(1)}, u32[]{:S(2)}, u32[]{:S(2)}) async-start(bf16[4,32,2048]{2,1,0:T(8,128)(2,1)} %bitcast.13), calls=%async_computation.1 | async-start | bytes 1048576 | tf_op jit(solution)/shard_map/all_to_all | solution.py:520
  44.7 8.8 %all-gather = f32[32,640]{1,0:T(8,128)S(1)} all-gather(f32[8,640]{1,0:T(8,128)S(1)} %get-tuple-element.39), channel_id=2, replica_groups=mesh['pipe'=32,'tensor'=4,'dp'=4] {'dp'}, dimensions={0}, use_global_device_ids=true | all-gather | bytes 102400 | tf_op jit(solution)/shard_map/all_gather | solution.py:521
  53.6 0.0 all-to-all-done.1.x_ref
  53.6 0.9 %finish.1 = (bf16[1,1,32,8192]{3,2,1,0:T(8,128)(2,1)}, f32[1,2,8]{2,1,0:T(2,128)}, f32[1,2,8]{2,1,0:T(2,128)}, f32[1,2,512]{2,1,0:T(2,128)}) custom-call(s32[1]{0:T(128)} %bitcast.me_ref.refs_0_, bf16[4,32,2048]{2,1,0:T(8,128)(2,1)S(1)} %all-to-all-done.1.x_ref, f32[4,8,640]{2,1,0:T(8,128)S(1)} %bitcast.6), custom_call_target="tpu_custom_call" | custom-call | flops 1000 | bytes 1000000 | tf_op jit(solution)/shard_map/finish/pallas_call | solution.py:523
Async XLA Ops:
  0.6 9.1 %copy-start = (f32[1,2,2048]{2,1,0:T(2,128)S(1)}, f32[1,2,2048]{2,1,0:T(2,128)}, u32[]{:S(2)}) copy-start(f32[1,2,2048]{2,1,0:T(2,128)} %gain_ref.3) | copy-start | bytes 49156
  0.6 9.1 %copy-start.3 = (f32[1,2,32]{2,1,0:T(2,128)S(1)}, f32[1,2,32]{2,1,0:T(2,128)}, u32[]{:S(2)}) copy-start(f32[1,2,32]{2,1,0:T(2,128)} %dskip_ref.3) | copy-start | bytes 772
  0.7 9.1 %copy-start.2 = (f32[1,2,32]{2,1,0:T(2,128)S(1)}, f32[1,2,32]{2,1,0:T(2,128)}, u32[]{:S(2)}) copy-start(f32[1,2,32]{2,1,0:T(2,128)} %alog_ref.3) | copy-start | bytes 772
  0.7 9.1 %copy-start.4 = (s32[2,1,1]{0,2,1:T(1,128)S(1)}, s32[2,1,1]{0,2,1:T(1,128)}, u32[]{:S(2)}) copy-start(s32[2,1,1]{0,2,1:T(1,128)} %param.21) | copy-start | bytes 28
  0.7 9.1 %copy-start.1 = (s32[2,1,1]{0,2,1:T(1,128)S(1)}, s32[2,1,1]{0,2,1:T(1,128)}, u32[]{:S(2)}) copy-start(s32[2,1,1]{0,2,1:T(1,128)} %param.20) | copy-start | bytes 28
  2.5 11.2 %all-to-all-start = ((bf16[4,32,2048]{2,1,0:T(8,128)(2,1)}), bf16[4,32,2048]{2,1,0:T(8,128)(2,1)S(1)}, u32[]{:S(2)}, u32[]{:S(2)}) async-start(bf16[4,32,2048]{2,1,0:T(8,128)(2,1)} %relay_out.1), calls=%async_computation | async-start | bytes 1048576 | tf_op jit(solution)/shard_map/all_to_all | solution.py:499
  15.1 23.4 %collective-permute-start = (bf16[128,2048]{1,0:T(8,128)(2,1)S(1)}, bf16[128,2048]{1,0:T(8,128)(2,1)S(1)}, u32[]{:S(2)}, u32[]{:S(2)}) collective-permute-start(bf16[128,2048]{1,0:T(8,128)(2,1)S(1)} %backward_first.1), channel_id=1, source_target_pairs={{16,0},{32,16},{48,32},{64,48},{80,64},{96,80},{112,96},{128,112},... | collective-permute-start | bytes 1572872 | tf_op jit(solution)/shard_map/ppermute | solution.py:21
  40.8 12.7 %all-to-all-start.1 = ((bf16[4,32,2048]{2,1,0:T(8,128)(2,1)}), bf16[4,32,2048]{2,1,0:T(8,128)(2,1)S(1)}, u32[]{:S(2)}, u32[]{:S(2)}) async-start(bf16[4,32,2048]{2,1,0:T(8,128)(2,1)} %bitcast.13), calls=%async_computation.1 | async-start | bytes 1048576 | tf_op jit(solution)/shard_map/all_to_all | solution.py:520
